TPU v7x, 128 devices: a whole 4x4x4 slice. The times are simulated.
128 devices in a mesh: dp: 32 (over x, y, core), heads: 4 (over z).
Axes of the slice: x: 4, y: 4, z: 4, core: 2. Of those that a mesh axis runs over, the one named last changes fastest.
Arguments:
- inputs: bfloat16 [96, 512, 768], P('dp', 'heads'), may hold values from -6 to 6
- key_mask: int32 [96, 512], P('dp'), may hold values from 0 to 1, as said below
- lengths: int32 [96], P('dp'), may hold values from 8 to 512, as said below
- cotangent: bfloat16 [96, 512, 768], P('dp', 'heads'), may hold values from -6 to 6
- query_weight: bfloat16 [768, 768], P(None, 'heads'), may hold values from -0.3125 to 0.3125
- w_key: bfloat16 [768, 768], P(None, 'heads'), may hold values from -0.21875 to 0.21875
- value_weight: bfloat16 [768, 768], P(None, 'heads'), may hold values from -0.21875 to 0.21875
- w_out: bfloat16 [768, 768], replicated, may hold values from -1.25 to 1.25
- w_inner: bfloat16 [768, 3072], replicated, may hold values from -0.21875 to 0.21875
- w_outer: bfloat16 [3072, 768], replicated, may hold values from -0.109375 to 0.109375
- gain_one: float32 [768], replicated, may hold values from 0.1 to 1.9
- shift_one: float32 [768], replicated, may hold values from -3 to 3
- gain_two: float32 [768], replicated, may hold values from 0.1 to 1.9
- shift_two: float32 [768], replicated, may hold values from -3 to 3
- down_query: bfloat16 [768, 8], replicated, may hold values from -0.21875 to 0.21875
- query_up_map: bfloat16 [8, 768], P(None, 'heads'), may hold values from -1 to 1
- down_value: bfloat16 [768, 8], replicated, may hold values from -0.21875 to 0.21875
- value_up_map: bfloat16 [8, 768], P(None, 'heads'), may hold values from -1 to 1
Outputs:
- activation: bfloat16 [96, 512, 768], P('dp', 'heads')
- input_grad: float32 [96, 512, 768], P('dp', 'heads')
- grad_down_query: float32 [768, 8], replicated
- grad_up_query: float32 [8, 768], P(None, 'heads')
- grad_down_value: float32 [768, 8], replicated
- grad_up_value: float32 [8, 768], P(None, 'heads')
Inputs may be any that keep to these rules, and one draw needn't show every extreme that they name: `lengths`: in each aligned block of 3 sentences one sentence, drawn from the seed, has length 512. `key_mask`: 1 only at positions below the sentence's length; position 0 is always 1.
All inputs are finite; a program needn't handle non-finite values.
Results may differ from a plain program's by a relative error of at most 0.019.
The roundings to bfloat16 on the way count: a program that leaves them out, or rounds other values in their place, can miss the bound.
Values may be sent and summed in bfloat16 or wider, within the bound.
A program may use at most 128 MiB of HBM per device.

v0:
```python
import functools
import math

import jax
import jax.numpy as jnp
from jax import lax
from jax.sharding import Mesh
from jax.sharding import PartitionSpec as P

HD = 64
DP_HEADS = ("dp_0", "dp_1", "dp_2", "heads")
DP = ("dp_0", "dp_1", "dp_2")


adapter_scale = 2.0


def in_order(tiles, dim):
    shape = list(tiles.shape[1:])
    shape[dim] *= tiles.shape[0]
    return jnp.moveaxis(tiles, 0, dim).reshape(shape)


def sent_to_all(value, axis):
    copies = jnp.broadcast_to(value, (lax.axis_size(axis), *value.shape))
    return lax.all_to_all(copies, axis, split_axis=0, concat_axis=0, tiled=True)


def gather_directly(value, axis, dim):
    return in_order(sent_to_all(value, axis), dim)


def in_blocks(value, dim, devices):
    shape = value.shape
    tiles = value.reshape(*shape[:dim], devices, shape[dim] // devices, *shape[dim + 1 :])
    return jnp.moveaxis(tiles, dim, 0)


def sent_and_summed(value, axis, dim):
    devices = lax.axis_size(axis)
    tiles = lax.all_to_all(in_blocks(value, dim, devices), axis, 0, 0, tiled=True)
    return jnp.sum(tiles.astype(jnp.float32), axis=0)


def side_by_side(arrays, axis, dim, along):
    widths = [a.shape[along] for a in arrays]
    both = jnp.concatenate(arrays, axis=along)
    result = sent_and_summed(both, axis, dim)
    return tuple(jnp.split(result, [sum(widths[:k]) for k in range(1, len(widths))], axis=along))


def by_axis(value, axes):
    return functools.reduce(lax.psum, axes, value)


def over_copies(value, axis):
    return sent_to_all(value, axis).sum(axis=0)


def in_one(arrays, axis):
    line, at, gathered = (jnp.concatenate([a.reshape(-1) for a in arrays]), 0, [])
    total = over_copies(line, axis)
    for a in arrays:
        gathered.append(total[at : at + a.size].reshape(a.shape))
        at += a.size
    return tuple(gathered)


def layer_norm(hidden, scale_gain, shift_bias):
    center = hidden - jnp.mean(hidden, axis=-1, keepdims=True)
    spread = jnp.mean(center * center, axis=-1, keepdims=True)
    return center * lax.rsqrt(spread + 1e-05) * scale_gain + shift_bias


def gelu_exact(inner_pre):
    return jax.nn.gelu(inner_pre, approximate=False)


def split_heads(rows_in_seq):
    return rows_in_seq.reshape(rows_in_seq.shape[0], rows_in_seq.shape[1] // HD, HD)


def masked_scores(query_rows, key_rows, key_keep):
    scores = jnp.einsum(
        "qhd,khd->hqk", query_rows, key_rows, preferred_element_type=jnp.float32
    ) * (1.0 / math.sqrt(HD))
    return jnp.where(key_keep[None, None, :] > 0, scores, -1e30)


def attend_forward(pieces):
    query_rows, key_rows, value_matrix_rows, key_keep = pieces
    length, columns = query_rows.shape
    scores = masked_scores(split_heads(query_rows), split_heads(key_rows), key_keep)
    row_max = jnp.max(scores, axis=-1, keepdims=True)
    raised = jnp.exp(scores - row_max)
    totals = jnp.sum(raised, axis=-1, keepdims=True)
    attention = (raised / totals).astype(jnp.bfloat16)
    context = jnp.einsum(
        "hqk,khd->qhd",
        attention,
        split_heads(value_matrix_rows),
        preferred_element_type=jnp.float32,
    )
    return (
        context.reshape(length, columns).astype(jnp.bfloat16),
        (row_max + jnp.log(totals))[:, :, 0],
    )


def attend_backward(pieces):
    query_rows, key_rows, value_matrix_rows, key_keep, log_total, grad_context = pieces
    length, columns = query_rows.shape
    scale_factor = 1.0 / math.sqrt(HD)
    query_heads = split_heads(query_rows)
    key_heads = split_heads(key_rows)
    grad_heads = split_heads(grad_context)
    scores = masked_scores(query_heads, key_heads, key_keep)
    attention = jnp.exp(scores - log_total[:, :, None])
    grad_attention = jnp.einsum(
        "qhd,khd->hqk",
        grad_heads,
        split_heads(value_matrix_rows),
        preferred_element_type=jnp.float32,
    )
    grad_values = jnp.einsum(
        "hqk,qhd->khd",
        attention.astype(jnp.bfloat16),
        grad_heads,
        preferred_element_type=jnp.float32,
    )
    inner_sum = jnp.sum(attention * grad_attention, axis=-1, keepdims=True)
    grad_scores = (attention * (grad_attention - inner_sum)).astype(jnp.bfloat16)
    grad_queries = (
        jnp.einsum("hqk,khd->qhd", grad_scores, key_heads, preferred_element_type=jnp.float32)
        * scale_factor
    )
    grad_keys = (
        jnp.einsum("hqk,qhd->khd", grad_scores, query_heads, preferred_element_type=jnp.float32)
        * scale_factor
    )
    return (
        grad_queries.reshape(length, columns).astype(jnp.bfloat16),
        grad_keys.reshape(length, columns).astype(jnp.bfloat16),
        grad_values.reshape(length, columns).astype(jnp.bfloat16),
    )


def per_device(
    inputs,
    key_mask,
    lengths,
    cotangent,
    query_weight,
    w_key,
    value_weight,
    w_out,
    w_inner,
    w_outer,
    gain_one,
    shift_one,
    gain_two,
    shift_two,
    down_query,
    query_up_map,
    down_value,
    value_up_map,
):
    seq_count, own_rows, features = inputs.shape
    head_index = lax.axis_index("heads")
    gathered = gather_directly(inputs, "heads", 1)
    length = gathered.shape[1]
    flattened_rows = gathered.reshape(seq_count * length, features)
    query_middle_rank = jnp.dot(
        flattened_rows, down_query, preferred_element_type=jnp.float32
    ).astype(jnp.bfloat16)
    value_middle_rank = jnp.dot(
        flattened_rows, down_value, preferred_element_type=jnp.float32
    ).astype(jnp.bfloat16)
    query_rows = (
        jnp.dot(flattened_rows, query_weight, preferred_element_type=jnp.float32)
        + adapter_scale
        * jnp.dot(query_middle_rank, query_up_map, preferred_element_type=jnp.float32)
    ).astype(jnp.bfloat16)
    key_rows = jnp.dot(flattened_rows, w_key, preferred_element_type=jnp.float32).astype(
        jnp.bfloat16
    )
    value_matrix_rows = (
        jnp.dot(flattened_rows, value_weight, preferred_element_type=jnp.float32)
        + adapter_scale
        * jnp.dot(value_middle_rank, value_up_map, preferred_element_type=jnp.float32)
    ).astype(jnp.bfloat16)
    columns = query_rows.shape[1]
    layout = (seq_count, length, columns)
    per_seq = (
        query_rows.reshape(layout),
        key_rows.reshape(layout),
        value_matrix_rows.reshape(layout),
        key_mask,
    )
    context, log_total = lax.map(attend_forward, per_seq)
    context_own = lax.all_to_all(context, "heads", split_axis=1, concat_axis=2, tiled=True)
    own_flat = context_own.reshape(seq_count * own_rows, features)
    own_inputs = inputs.reshape(seq_count * own_rows, features)
    first_sum = own_inputs.astype(jnp.float32) + jnp.dot(
        own_flat, w_out, preferred_element_type=jnp.float32
    )
    normed_one, norm_one_back = jax.vjp(
        lambda hidden: layer_norm(hidden, gain_one, shift_one), first_sum
    )
    inner_pre = jnp.dot(
        normed_one.astype(jnp.bfloat16), w_inner, preferred_element_type=jnp.float32
    )
    active, gelu_back = jax.vjp(gelu_exact, inner_pre)
    branch_out = jnp.dot(active.astype(jnp.bfloat16), w_outer, preferred_element_type=jnp.float32)
    final_norm, norm_two_back = jax.vjp(
        lambda hidden: layer_norm(hidden, gain_two, shift_two), normed_one + branch_out
    )
    activation = final_norm.reshape(seq_count, own_rows, features).astype(jnp.bfloat16)
    position = head_index * own_rows + jnp.arange(own_rows, dtype=jnp.int32)
    row_valid = (position[None, :] < lengths[:, None]).astype(jnp.float32)
    tangent = (cotangent.astype(jnp.float32) * row_valid[:, :, None]).reshape(
        seq_count * own_rows, features
    )
    grad_second = norm_two_back(tangent)[0]
    grad_active = jnp.dot(
        grad_second.astype(jnp.bfloat16), w_outer.T, preferred_element_type=jnp.float32
    )
    grad_inner = gelu_back(grad_active)[0].astype(jnp.bfloat16)
    grad_normed = grad_second + jnp.dot(grad_inner, w_inner.T, preferred_element_type=jnp.float32)
    grad_first = norm_one_back(grad_normed)[0]
    grad_context = (
        jnp.dot(grad_first.astype(jnp.bfloat16), w_out.T, preferred_element_type=jnp.float32)
        .astype(jnp.bfloat16)
        .reshape(seq_count, own_rows, features)
    )
    grad_heads = lax.all_to_all(grad_context, "heads", split_axis=2, concat_axis=1, tiled=True)
    grad_queries, grad_keys, grad_values = lax.map(
        attend_backward, per_seq + (log_total, grad_heads)
    )
    rank_width = query_middle_rank.shape[1]
    flat_queries = grad_queries.reshape(seq_count * length, columns)
    flat_values = grad_values.reshape(seq_count * length, columns)
    query_up_gradient = adapter_scale * jnp.dot(
        query_middle_rank.T, flat_queries, preferred_element_type=jnp.float32
    )
    value_up_gradient = adapter_scale * jnp.dot(
        value_middle_rank.T, flat_values, preferred_element_type=jnp.float32
    )
    flat_keys = grad_keys.reshape(seq_count * length, columns)
    query_middle_piece = adapter_scale * jnp.dot(
        flat_queries, query_up_map.T, preferred_element_type=jnp.float32
    )
    value_middle_piece = adapter_scale * jnp.dot(
        flat_values, value_up_map.T, preferred_element_type=jnp.float32
    )
    input_part = jnp.dot(flat_queries, query_weight.T, preferred_element_type=jnp.float32)
    input_part = input_part + jnp.dot(flat_keys, w_key.T, preferred_element_type=jnp.float32)
    input_part = input_part + jnp.dot(
        flat_values, value_weight.T, preferred_element_type=jnp.float32
    )
    input_heads, mid_query_sum, mid_value_sum = side_by_side(
        (
            input_part.reshape(seq_count, length, features).astype(jnp.bfloat16),
            query_middle_piece.reshape(seq_count, length, -1).astype(jnp.bfloat16),
            value_middle_piece.reshape(seq_count, length, -1).astype(jnp.bfloat16),
        ),
        "heads",
        1,
        2,
    )
    input_heads = input_heads.reshape(seq_count * own_rows, features)
    mid_query_low = mid_query_sum.reshape(seq_count * own_rows, rank_width).astype(jnp.bfloat16)
    mid_value_low = mid_value_sum.reshape(seq_count * own_rows, rank_width).astype(jnp.bfloat16)
    input_grad = grad_first + input_heads
    input_grad = input_grad + jnp.dot(
        mid_query_low, down_query.T, preferred_element_type=jnp.float32
    )
    input_grad = input_grad + jnp.dot(
        mid_value_low, down_value.T, preferred_element_type=jnp.float32
    )
    down_query_grad = jnp.dot(own_inputs.T, mid_query_low, preferred_element_type=jnp.float32)
    down_value_grad = jnp.dot(own_inputs.T, mid_value_low, preferred_element_type=jnp.float32)
    down_query_grad, down_value_grad = (
        by_axis(down_query_grad, DP_HEADS),
        by_axis(down_value_grad, DP_HEADS),
    )
    query_up_gradient, value_up_gradient = in_one((query_up_gradient, value_up_gradient), DP)
    return (
        activation,
        input_grad.reshape(seq_count, own_rows, features),
        down_query_grad,
        query_up_gradient,
        down_value_grad,
        value_up_gradient,
    )


def solution(mesh):
    finer = Mesh(
        mesh.devices.reshape(4, 4, 2, mesh.shape["heads"]), ("dp_0", "dp_1", "dp_2", "heads")
    )
    in_specs = (
        P(DP, "heads", None),
        P(DP, None),
        P(DP),
        P(DP, "heads", None),
        P(None, "heads"),
        P(None, "heads"),
        P(None, "heads"),
        P(),
        P(),
        P(),
        P(),
        P(),
        P(),
        P(),
        P(),
        P(None, "heads"),
        P(),
        P(None, "heads"),
    )
    out_specs = (
        P(DP, "heads", None),
        P(DP, "heads", None),
        P(),
        P(None, "heads"),
        P(),
        P(None, "heads"),
    )
    return jax.shard_map(
        per_device, mesh=finer, in_specs=in_specs, out_specs=out_specs, check_vma=False
    )
```

profile of v0, /device:TPU:0, one launch (start us, length us, event | category | flops | bytes accessed | tf_op | source)
XLA Modules:
  0.0 283.8 jit_solution(10320153994940405803)
XLA Ops:
  0.6 2.8 broadcast_in_dim.66
  3.4 5.4 %all-to-all-start = ((bf16[4,3,128,768]{3,2,1,0:T(8,128)(2,1)}), bf16[4,3,128,768]{3,2,1,0:T(8,128)(2,1)}, u32[]{:S(2)}, u32[]{:S(2)}) async-start(bf16[4,3,128,768]{3,2,1,0:T(8,128)(2,1)} %broadcast_in_dim.66), calls=%async_computation | async-start | bytes 4718592 | tf_op jit(solution)/shard_map/all_to_all | solution.py:26
  8.8 29.5 %all-to-all-done = bf16[4,3,128,768]{3,2,1,0:T(8,128)(2,1)} async-done(((bf16[4,3,128,768]{3,2,1,0:T(8,128)(2,1)}), bf16[4,3,128,768]{3,2,1,0:T(8,128)(2,1)}, u32[]{:S(2)}, u32[]{:S(2)}) %all-to-all-start) | async-done | bytes 2359328 | tf_op jit(solution)/shard_map/all_to_all | solution.py:26
  38.3 1.8 copy.129
  45.5 9.5 %while.26 = (s32[]{:T(128)}, bf16[3,512,192]{1,2,0:T(8,128)(2,1)S(1)}, f32[3,3,512]{2,1,0:T(4,128)}, bf16[3,512,192]{1,2,0:T(8,128)(2,1)S(1)}, s32[3,512]{1,0:T(...) while((s32[]{:T(128)}, bf16[3,512,192]{1,2,0:T(8,128)(2,1)S(1)}, ...), condition=%wide.region_3.4_spmd, body=%wide.region_0.3_spmd.sunk | while | flops 210861056 | bytes 11852389 | solution.py:200
  47.7 1.0 fusion.138
  50.9 1.0 fusion.138
  54.1 1.0 fusion.138
  55.1 1.4 copy.133
  56.5 4.4 %all-to-all-start.1 = ((bf16[3,512,192]{2,0,1:T(4,128)(2,1)}), bf16[3,512,192]{2,0,1:T(4,128)(2,1)}, u32[]{:S(2)}, u32[]{:S(2)}) async-start(bf16[3,512,192]{2,0,1:T(4,128)(2,1)} %copy.133), calls=%async_computation.1 | async-start | bytes 2097152 | tf_op jit(solution)/shard_map/all_to_all | solution.py:201
  61.0 2.3 convert_multiply_fusion
  63.3 11.7 %all-to-all-done.1 = bf16[3,512,192]{2,0,1:T(4,128)(2,1)} async-done(((bf16[3,512,192]{2,0,1:T(4,128)(2,1)}), bf16[3,512,192]{2,0,1:T(4,128)(2,1)}, u32[]{:S(2)}, u32[]{:S(2)}) %all-to-all-start.1) | async-done | bytes 589856 | tf_op jit(solution)/shard_map/all_to_all | solution.py:201
  75.0 2.9 %copy.180 = bf16[3,4,128,192]{3,1,2,0:T(4,128)(2,1)} copy(bf16[3,4,128,192]{3,0,2,1:T(4,128)(2,1)} %bitcast.21) | data formatting | bytes 1179648 | tf_op jit(solution)/shard_map/all_to_all | solution.py:201
  77.9 2.6 reshape.312
  80.5 2.1 fusion.53
  83.5 13.2 %fusion.13 = (f32[384,3072]{1,0:T(8,128)S(1)}, f32[384,3072]{1,0:T(8,128)S(1)}) fusion(bf16[768,3072]{1,0:T(8,128)(2,1)} %param.30, f32[384,768]{1,0:T(8,128)S(1)} %get-tuple-element.267, f32[768]{0:T(1024)} %param.33, f32[768]{0:T(1024)} %param.32, f32[384]{0:T(512)S(1)} %fusion.44, f32[384]{0:T(512)S(1)} %broadcast_multiply_fusion.1), kind=kOutput, calls=%fused_computation.37 | convolution fusion | flops 1886552064 | bytes 15344640 | tf_op jit(solution)/shard_map/dot_general | solution.py:210
  96.7 2.2 fusion.54
  98.9 1.3 copy-done.6
  100.7 1.7 fusion.51
  103.1 12.9 %multiply_reduce_fusion.1 = (f32[384]{0:T(512)}, f32[384,768]{1,0:T(8,128)}) fusion(f32[384,768]{1,0:T(8,128)S(1)} %get-tuple-element.267, f32[384]{0:T(512)S(1)} %broadcast_multiply_fusion.1, f32[768]{0:T(1024)} %param.32, bf16[768,3072]{1,0:T(8,128)(2,1)} %param.30, f32[384,3072]{1,0:T(8,128)} %copy-done.5, f32[384,3072]{1,0:T(8,128)} %copy-done.6, ...), kind=kOutput, calls=%fused_computation.82 | convolution fusion | flops 3642752512 | bytes 22420992 | tf_op jit(solution)/shard_map/dot_general | solution.py:229
  116.7 1.7 fusion.50
  118.4 1.0 copy-done.7
  119.4 1.5 convolution_convert_fusion.3
  120.9 1.5 copy.135
  122.4 12.8 %all_to_all.49 = bf16[3,128,768]{1,0,2:T(4,128)(2,1)S(1)} all-to-all(bf16[3,128,768]{1,0,2:T(4,128)(2,1)S(1)} %copy.135), channel_id=1, replica_groups=mesh['dp_0'=4,'dp_1'=4,'dp_2'=2,'heads'=4] {'heads'}, dimensions={2} | all-to-all | bytes 1179648 | tf_op jit(solution)/shard_map/all_to_all | solution.py:236
  137.2 20.2 %while.27 = (s32[]{:T(128)}, bf16[3,512,192]{1,2,0:T(8,128)(2,1)S(1)}, bf16[3,512,192]{1,2,0:T(8,128)(2,1)}, bf16[3,512,192]{1,2,0:T(8,128)(2,1)}, bf16[3,512,19...) while((s32[]{:T(128)}, ...), condition=%wide.region_14.15_spmd, body=%wide.region_12.14_spmd.sunk | while | flops 510884864 | bytes 28345992 | solution.py:237
  139.6 1.1 multiply_reduce_fusion.6
  146.3 1.1 multiply_reduce_fusion.6
  153.1 1.1 multiply_reduce_fusion.6
  157.5 1.0 convolution_multiply_fusion.7
  158.5 4.0 %fusion.58 = f32[1536,768]{1,0:T(8,128)} fusion(bf16[1536,192]{0,1:T(8,128)(2,1)S(1)} %bitcast.207, bf16[768,192]{0,1:T(8,128)(2,1)} %param.26), kind=kOutput, calls=%fused_computation.138 | convolution fusion | flops 452984832 | bytes 5603328 | tf_op jit(solution)/shard_map/dot_general | solution.py:256
  163.1 1.0 broadcast_in_dim.71
  164.1 7.3 %all-to-all-start.4 = ((f32[32,1,3072]{2,1,0:T(1,128)}), f32[32,1,3072]{2,1,0:T(1,128)S(1)}, u32[]{:S(2)}, u32[]{:S(2)}) async-start(f32[32,1,3072]{2,1,0:T(1,128)} %broadcast_in_dim.71), calls=%async_computation.4 | async-start | bytes 786432 | tf_op jit(solution)/shard_map/all_to_all | solution.py:26
  171.5 1.9 fusion.59
  174.0 2.3 add_convert_fusion
  176.4 4.3 %copy.144 = bf16[3,4,128,768]{2,3,0,1:T(8,128)(2,1)} copy(bf16[3,4,128,768]{3,2,1,0:T(8,128)(2,1)} %bitcast.213) | data formatting | bytes 4718592 | tf_op jit(solution)/shard_map/convert_element_type | solution.py:263
  180.7 3.3 %maximum_bitcast_fusion = bf16[4,3,128,784]{2,3,1,0:T(8,128)(2,1)} fusion(bf16[3,4,128,768]{2,3,0,1:T(8,128)(2,1)} %copy.144, bf16[3,4,128,8]{2,3,1,0:T(8,128)(2,1)S(1)} %bitcast.232, bf16[3,4,128,8]{2,3,1,0:T(8,128)(2,1)S(1)} %bitcast.233), kind=kLoop, calls=%fused_computation.61 | loop fusion | flops 7225344 | bytes 4816896 | tf_op jit(solution)/shard_map/transpose | solution.py:36
  184.0 4.5 %all-to-all-start.3 = ((bf16[4,3,128,784]{2,3,1,0:T(8,128)(2,1)}), bf16[4,3,128,784]{2,3,1,0:T(8,128)(2,1)}, u32[]{:S(2)}, u32[]{:S(2)}) async-start(bf16[4,3,128,784]{2,3,1,0:T(8,128)(2,1)} %maximum_bitcast_fusion), calls=%async_computation.3 | async-start | bytes 4816896 | tf_op jit(solution)/shard_map/all_to_all | solution.py:41
  190.1 28.8 %all-to-all-done.3 = bf16[4,3,128,784]{2,3,1,0:T(8,128)(2,1)} async-done(((bf16[4,3,128,784]{2,3,1,0:T(8,128)(2,1)}), bf16[4,3,128,784]{2,3,1,0:T(8,128)(2,1)}, u32[]{:S(2)}, u32[]{:S(2)}) %all-to-all-start.3) | async-done | bytes 2408480 | tf_op jit(solution)/shard_map/all_to_all | solution.py:41
  219.0 2.2 convert_reduce_fusion
  222.8 1.1 split.12
  223.9 1.6 copy.161
  225.8 1.1 convolution_add_fusion.2
  226.9 2.1 convolution_add_fusion.1
  229.0 17.6 %all-reduce.2 = (f32[768,8]{0,1:T(8,128)S(1)}, f32[768,8]{0,1:T(8,128)S(1)}) all-reduce(f32[768,8]{0,1:T(8,128)S(1)} %copy-done.19, f32[768,8]{0,1:T(8,128)S(1)} %copy-done.18), channel_id=1, replica_groups=mesh['dp_0'=4,'dp_1'=4,'dp_2'=2,'heads'=4] {'dp_0'}, use_global_device_ids=true, to_apply=%region_16.17 | all-reduce | flops 12288 | bytes 98304 | tf_op jit(solution)/shard_map/psum | solution.py:53
  246.5 17.4 %all-reduce.1 = (f32[768,8]{0,1:T(8,128)S(1)}, f32[768,8]{0,1:T(8,128)S(1)}) all-reduce(f32[768,8]{0,1:T(8,128)S(1)} %get-tuple-element.245, f32[768,8]{0,1:T(8,128)S(1)} %get-tuple-element.246), channel_id=1, replica_groups=mesh['dp_0'=4,'dp_1'=4,'dp_2'=2,'heads'=4] {'dp_1'}, use_global_device_ids=true, to_apply=%region_17.18 | all-reduce | flops 12288 | bytes 98304 | tf_op jit(solution)/shard_map/psum | solution.py:53
  263.9 3.5 %all-reduce.3 = (f32[768,8]{0,1:T(8,128)S(1)}, f32[768,8]{0,1:T(8,128)S(1)}) all-reduce(f32[768,8]{0,1:T(8,128)S(1)} %get-tuple-element.243, f32[768,8]{0,1:T(8,128)S(1)} %get-tuple-element.244), channel_id=1, replica_groups=mesh['dp_0'=4,'dp_1'=4,'dp_2'=2,'heads'=4] {'dp_2'}, use_global_device_ids=true, to_apply=%region_18.19 | all-reduce | flops 12288 | bytes 98304 | tf_op jit(solution)/shard_map/psum | solution.py:53
  267.4 16.4 %all-reduce = (f32[768,8]{0,1:T(8,128)}, f32[768,8]{0,1:T(8,128)}) all-reduce(f32[768,8]{0,1:T(8,128)S(1)} %get-tuple-element.247, f32[768,8]{0,1:T(8,128)S(1)} %get-tuple-element.248), channel_id=1, replica_groups=mesh['dp_0'=4,'dp_1'=4,'dp_2'=2,'heads'=4] {'heads'}, use_global_device_ids=true, to_apply=%region_19.20 | all-reduce | flops 12288 | bytes 98304 | tf_op jit(solution)/shard_map/psum | solution.py:53
  (186 shorter events, 38.0 us)
Async XLA Ops:
  0.6 79.9 %copy-start = (bf16[768,768]{1,0:T(8,128)(2,1)S(1)}, bf16[768,768]{1,0:T(8,128)(2,1)}, u32[]{:S(2)}) copy-start(bf16[768,768]{1,0:T(8,128)(2,1)} %param.29) | copy-start | bytes 3538948
  3.4 34.9 %all-to-all-start = ((bf16[4,3,128,768]{3,2,1,0:T(8,128)(2,1)}), bf16[4,3,128,768]{3,2,1,0:T(8,128)(2,1)}, u32[]{:S(2)}, u32[]{:S(2)}) async-start(bf16[4,3,128,768]{3,2,1,0:T(8,128)(2,1)} %broadcast_in_dim.66), calls=%async_computation | async-start | bytes 4718592 | tf_op jit(solution)/shard_map/all_to_all | solution.py:26
  8.8 31.3 %copy-start.21 = (bf16[768,8]{0,1:T(8,128)(2,1)S(1)}, bf16[768,8]{0,1:T(8,128)(2,1)}, u32[]{:S(2)}) copy-start(bf16[768,8]{0,1:T(8,128)(2,1)} %param.36) | copy-start | bytes 36868
  8.8 32.0 %copy-start.11 = (bf16[768,192]{0,1:T(8,128)(2,1)S(1)}, bf16[768,192]{0,1:T(8,128)(2,1)}, u32[]{:S(2)}) copy-start(bf16[768,192]{0,1:T(8,128)(2,1)} %param.26) | copy-start | bytes 884740
  40.8 4.1 %copy-start.17 = (bf16[1536,8]{0,1:T(8,128)(2,1)}, bf16[1536,8]{0,1:T(8,128)(2,1)S(1)}, u32[]{:S(2)}) copy-start(bf16[1536,8]{0,1:T(8,128)(2,1)S(1)} %convolution_convert_fusion.1) | copy-start | bytes 73732
  40.8 1.0 copy-start.14
  41.8 0.9 copy-start.23
  41.8 1.6 copy-start.12
  43.5 1.3 copy-start.15
  43.5 1.0 copy-start.30
  43.5 1.4 copy-start.28
  44.8 0.7 copy-start.20
  55.1 22.8 %copy-start.1 = (bf16[3,512,192]{1,2,0:T(8,128)(2,1)}, bf16[3,512,192]{1,2,0:T(8,128)(2,1)S(1)}, u32[]{:S(2)}) copy-start(bf16[3,512,192]{1,2,0:T(8,128)(2,1)S(1)} %get-tuple-element.455) | copy-start | bytes 1769476
  55.1 5.9 %copy-start.36 = (s32[3]{0:T(128)S(1)}, s32[3]{0:T(128)}, u32[]{:S(2)}) copy-start(s32[3]{0:T(128)} %param.24) | copy-start | bytes 40
  56.5 18.5 %all-to-all-start.1 = ((bf16[3,512,192]{2,0,1:T(4,128)(2,1)}), bf16[3,512,192]{2,0,1:T(4,128)(2,1)}, u32[]{:S(2)}, u32[]{:S(2)}) async-start(bf16[3,512,192]{2,0,1:T(4,128)(2,1)} %copy.133), calls=%async_computation.1 | async-start | bytes 2097152 | tf_op jit(solution)/shard_map/all_to_all | solution.py:201
  80.5 16.1 %slice-start.2 = ((s8[4718592]{0:T(1024)(128)(4,1)}), s8[4194304]{0:T(1024)(128)(4,1)S(1)}, s32[]{:S(2)}) async-start(s8[4718592]{0:T(1024)(128)(4,1)} %bitcast.218), calls=%async_computation.7 | async-start | bytes 8388608
  82.9 0.5 copy-start.27
  83.4 13.2 %slice-start.3 = ((s8[4718592]{0:T(1024)(128)(4,1)}), s8[524288]{0:T(1024)(128)(4,1)S(1)}, s32[]{:S(2)}) async-start(s8[4718592]{0:T(1024)(128)(4,1)} %bitcast.218), calls=%async_computation.8 | async-start | bytes 1048576
  83.4 13.2 %copy-start.25 = (f32[768]{0:T(1024)S(1)}, f32[768]{0:T(1024)}, u32[]{:S(2)}) copy-start(f32[768]{0:T(1024)} %param.33) | copy-start | bytes 9220
  83.5 13.2 %copy-start.26 = (f32[768]{0:T(1024)S(1)}, f32[768]{0:T(1024)}, u32[]{:S(2)}) copy-start(f32[768]{0:T(1024)} %param.32) | copy-start | bytes 9220
  96.6 2.3 copy-start.5
  96.6 3.6 %copy-start.6 = (f32[384,3072]{1,0:T(8,128)}, f32[384,3072]{1,0:T(8,128)S(1)}, u32[]{:S(2)}) copy-start(f32[384,3072]{1,0:T(8,128)S(1)} %get-tuple-element.269) | copy-start | bytes 14155780
  96.7 3.6 %copy-start.2 = (f32[3,128,768]{2,1,0:T(8,128)S(1)}, f32[3,128,768]{2,1,0:T(8,128)}, u32[]{:S(2)}) copy-start(f32[3,128,768]{2,1,0:T(8,128)} %convert_multiply_fusion) | copy-start | bytes 3538948
  96.7 3.6 %copy-start.32 = (f32[768]{0:T(1024)S(1)}, f32[768]{0:T(1024)}, u32[]{:S(2)}) copy-start(f32[768]{0:T(1024)} %param.34) | copy-start | bytes 9220
  96.7 4.0 %copy-start.35 = (f32[768]{0:T(1024)S(1)}, f32[768]{0:T(1024)}, u32[]{:S(2)}) copy-start(f32[768]{0:T(1024)} %param.35) | copy-start | bytes 9220
  118.4 1.1 copy-start.7
  118.4 2.5 copy-start.33
  158.4 4.0 %copy-start.29 = (bf16[8,192]{1,0:T(8,128)(2,1)S(1)}, bf16[8,192]{1,0:T(8,128)(2,1)}, u32[]{:S(2)}) copy-start(bf16[8,192]{1,0:T(8,128)(2,1)} %param.37) | copy-start | bytes 9220
  158.4 4.3 %copy-start.10 = (bf16[3,512,192]{1,2,0:T(8,128)(2,1)S(1)}, bf16[3,512,192]{1,2,0:T(8,128)(2,1)}, u32[]{:S(2)}) copy-start(bf16[3,512,192]{1,2,0:T(8,128)(2,1)} %get-tuple-element.102) | copy-start | bytes 1769476
  158.4 4.3 %copy-start.16 = (bf16[1536,8]{0,1:T(8,128)(2,1)S(1)}, bf16[1536,8]{0,1:T(8,128)(2,1)}, u32[]{:S(2)}) copy-start(bf16[1536,8]{0,1:T(8,128)(2,1)} %copy-done.15) | copy-start | bytes 73732
  162.5 9.0 %copy-start.9 = (bf16[3,512,192]{1,2,0:T(8,128)(2,1)S(1)}, bf16[3,512,192]{1,2,0:T(8,128)(2,1)}, u32[]{:S(2)}) copy-start(bf16[3,512,192]{1,2,0:T(8,128)(2,1)} %get-tuple-element.101) | copy-start | bytes 1769476
  164.1 19.9 %all-to-all-start.4 = ((f32[32,1,3072]{2,1,0:T(1,128)}), f32[32,1,3072]{2,1,0:T(1,128)S(1)}, u32[]{:S(2)}, u32[]{:S(2)}) async-start(f32[32,1,3072]{2,1,0:T(1,128)} %broadcast_in_dim.71), calls=%async_computation.4 | async-start | bytes 786432 | tf_op jit(solution)/shard_map/all_to_all | solution.py:26
  171.5 2.3 slice-start
  171.5 2.4 slice-start.1
  171.5 2.4 copy-start.13
  174.0 2.3 copy-start.31
  184.0 35.0 %all-to-all-start.3 = ((bf16[4,3,128,784]{2,3,1,0:T(8,128)(2,1)}), bf16[4,3,128,784]{2,3,1,0:T(8,128)(2,1)}, u32[]{:S(2)}, u32[]{:S(2)}) async-start(bf16[4,3,128,784]{2,3,1,0:T(8,128)(2,1)} %maximum_bitcast_fusion), calls=%async_computation.3 | async-start | bytes 4816896 | tf_op jit(solution)/shard_map/all_to_all | solution.py:41
  188.5 32.6 %copy-start.3 = (bf16[3,128,768]{2,1,0:T(8,128)(2,1)S(1)}, bf16[3,128,768]{2,1,0:T(8,128)(2,1)}, u32[]{:S(2)}) copy-start(bf16[3,128,768]{2,1,0:T(8,128)(2,1)} %param.22) | copy-start | bytes 1769476
  221.1 1.6 copy-start.4
  221.2 4.4 %copy-start.8 = (f32[384,768]{1,0:T(8,128)S(1)}, f32[384,768]{1,0:T(8,128)}, u32[]{:S(2)}) copy-start(f32[384,768]{1,0:T(8,128)} %copy-done.7) | copy-start | bytes 3538948
  221.2 4.4 %copy-start.34 = (f32[384]{0:T(512)S(1)}, f32[384]{0:T(512)}, u32[]{:S(2)}) copy-start(f32[384]{0:T(512)} %copy-done.33) | copy-start | bytes 4612
  223.9 1.9 copy-start.22
  225.6 1.3 copy-start.24
  225.8 3.2 %copy-start.18 = (f32[768,8]{0,1:T(8,128)S(1)}, f32[768,8]{0,1:T(8,128)}, u32[]{:S(2)}) copy-start(f32[768,8]{0,1:T(8,128)} %convolution_bitcast_fusion) | copy-start | bytes 73732
  225.8 3.2 %copy-start.19 = (f32[768,8]{0,1:T(8,128)S(1)}, f32[768,8]{0,1:T(8,128)}, u32[]{:S(2)}) copy-start(f32[768,8]{0,1:T(8,128)} %convolution_bitcast_fusion.1) | copy-start | bytes 73732
where the time goes:
time: 285 us; the launch traced here: 284 us
  waiting for transfers between devices  70 us (25%)
  blocking collectives  67.6 us (24%)
  matrix products  66.4 us (23%)
  local copies, waits for them, and re-layouts  36.4 us (13%)
  starting transfers between devices  21.7 us (8%)
  other arithmetic  20.2 us (7%)
    psum x4, blocking collectives, by_axis(): return functools.reduce(lax.psum, axes, value)  54.8 us
    all_to_all x2, waiting for transfers between devices, sent_to_all(): return lax.all_to_all(copies, axis, split_axis=0, concat_axis=0, tiled=True)  29.5 us
    all_to_all x1, waiting for transfers between devices, sent_and_summed(): lax.all_to_all(in_blocks(value, dim, devices), axis, 0, 0, tiled=True)  28.8 us
    dot_general x1, matrix products, per_device(): jnp.dot(normed_one.astype(jnp.bfloat16), w_inner, preferred_element_type=...  13.2 us
    dot_general x1, matrix products, per_device(): jnp.dot(grad_inner, w_inner.T, preferred_element_type=jnp.float32)  12.9 us
    all_to_all x1, blocking collectives, per_device(): lax.all_to_all(grad_context, 'heads', split_axis=2, concat_axis=1, tiled=...  12.8 us
    all_to_all x2, starting transfers between devices, sent_to_all(): return lax.all_to_all(copies, axis, split_axis=0, concat_axis=0, tiled=True)  12.7 us
    all_to_all x1, waiting for transfers between devices, per_device(): lax.all_to_all(context, 'heads', split_axis=1, concat_axis=2, tiled=True)  11.7 us
  transfers between devices with their start and end apart: 4, of which 3 were waited for; matrix products, arithmetic and copies ran while one was open for 6% of the time, Pallas kernels for 0%

commit v1 on v0

v1 whole, which is shorter than its diff:
```python
import functools

import jax
import jax.numpy as jnp
from jax import lax
from jax.experimental import pallas as pl
from jax.experimental.pallas import tpu as pltpu
from jax.sharding import Mesh
from jax.sharding import PartitionSpec as P

BF, F32 = jnp.bfloat16, jnp.float32
S, D, FF, HD, G = 512, 768, 3072, 64, 4
B, Q = 3, 128
GW = 640
C = 256
NT = (((1,), (1,)), ((), ()))
DP = ("dp_0", "dp_1", "dp_2")
MESH = pl.DeviceIdType.MESH
LANES = ((0, 384), (384, 256))


def nn(a, b):
    return jnp.dot(a, b, preferred_element_type=F32)


def nt(a, b):
    return lax.dot_general(a, b, NT, preferred_element_type=F32)


def project(g, x, wg, up, bias, knat, vnat, yt):
    xv = x[...]
    tail = nn(xv, wg[g, :, 384:GW])
    lane = lax.broadcasted_iota(jnp.int32, (S, 256), 1)
    kb = jnp.where(lane == 255, bias[...], tail).astype(BF)
    knat[g] = kb
    qv = nn(xv, wg[g, :, 0:384]) + nn(kb[:, 128:256], up[g])
    lane2 = lax.broadcasted_iota(jnp.int32, (S, 384), 1)
    qvb = qv.astype(BF)
    vnat[g] = qvb[:, 128:384]
    qvs = jnp.where(lane2 < 192, qvb * 0.125, qvb).astype(BF)
    yt[g, 0:384, :] = qvs.T
    yt[g, 384:GW, :] = kb.T


def pad_rows(piece, before, total):
    parts = []
    if before:
        parts.append(jnp.zeros((before, S), BF))
    parts.append(piece)
    after = total - before - piece.shape[0]
    if after:
        parts.append(jnp.zeros((after, S), BF))
    return jnp.concatenate(parts, axis=0)


def attend(g, knat, yt, sscr, p, rl, ctxt):
    one_row = (lax.broadcasted_iota(jnp.int32, (64, S), 0) == 63).astype(BF)
    ones = jnp.ones((16, S), BF)
    kb = knat[g]
    for j in range(3):
        rhs = jnp.concatenate([pad_rows(yt[g, 64 * j : 64 * j + 64, :], 64 * j, 192), one_row], axis=0)
        for half in range(2):
            cols = slice(256 * half, 256 * half + 256)
            s = nn(kb, rhs[:, cols])
            sscr[j, half] = s
            m = jnp.max(s, axis=0, keepdims=True)
            p[g * 3 + j, :, cols] = jnp.exp(sscr[j, half] - m).astype(BF)
        vt = jnp.concatenate([yt[g, 192 + 64 * j : 256 + 64 * j, :], ones], axis=0)
        ot = nn(vt, p[g * 3 + j])
        rinv = 1.0 / ot[64:65]
        rl[g * 3 + j] = rinv
        ctxt[g, 64 * j : 64 * j + 64, :] = (ot[0:64] * rinv).astype(BF)


def attend_back(g, vnat, yt, p, rl, ctxt, dot_ref, dsscr, dyt):
    vb = vnat[g]
    for j in range(3):
        h = g * 3 + j
        rows = slice(64 * j, 64 * j + 64)
        do = (dot_ref[g, rows, :] * rl[h]).astype(BF)
        dsum = jnp.sum(do.astype(F32) * ctxt[g, rows, :].astype(F32), axis=0, keepdims=True)
        rhs = pad_rows(do, 64 + 64 * j, 256)
        for half in range(2):
            cols = slice(256 * half, 256 * half + 256)
            dp = nn(vb, rhs[:, cols])
            dsscr[j, :, cols] = (p[h, :, cols].astype(F32) * (dp - dsum[:, cols])).astype(BF)
        dyt[g, 192 + 64 * j : 256 + 64 * j, :] = nt(do, p[h]).astype(BF)
        ds = dsscr[j]
        dyt[g, 384 + 64 * j : 448 + 64 * j, :] = nt(yt[g, rows, :], ds).astype(BF)
        dyt[g, rows, :] = (nn(yt[g, 384 + 64 * j : 448 + 64 * j, :], ds) * 0.125).astype(BF)


def gelu_pair(v):
    e = jnp.exp(v * v * -0.5)
    t = 1.0 / (1.0 + 0.23164189 * jnp.abs(v))
    tail = t * (0.127414796 + t * (-0.142248368 + t * (0.7107068705 + t * (-0.7265760135 + t * 0.5307027145)))) * e
    cdf = jnp.where(v >= 0.0, 1.0 - tail, tail)
    return v * cdf, cdf + v * (e * 0.3989422804)


def norm(h):
    mean = jnp.mean(h, axis=-1, keepdims=True)
    c = h - mean
    r = lax.rsqrt(jnp.mean(c * c, axis=-1, keepdims=True) + 1e-5)
    return c * r, r


def norm_back(n, xhat, r):
    return r * (n - jnp.mean(n, axis=-1, keepdims=True) - xhat * jnp.mean(n * xhat, axis=-1, keepdims=True))


def remote(src, dst, send, recv, **where):
    return pltpu.make_async_remote_copy(
        src_ref=src, dst_ref=dst, send_sem=send, recv_sem=recv, device_id=where, device_id_type=MESH
    )


def layer(
    inputs, cot, kmask, lengths, wq, wk, wv, w_out, w_inner, w_outer, g1, b1, g2, b2, dq, uq, dv, uv,
    act_out, ig_out, gd_out, gu_out,
    x, ct, wqs, wks, wvs, wo, wi, wt, wg, up, act, igb,
    bias, knat, vnat, yt, sscr, p, rl, ctxt, xhat1, r1s, n1b, dact, acc, dot_ref, dsscr, dyt, gnb,
    msg, redz, redc, redx, redy, gdp,
    lsem, xsem, csem, wsem, usem, w1, w2, w3, asem, isem, gz, gc, gx, gy, gf,
):
    ix, iy, ic, iz = (lax.axis_index(a) for a in ("dp_0", "dp_1", "dp_2", "heads"))
    rank = lax.rem(iz + 2 * ic, 4)
    owner = rank < 3
    mine = jnp.minimum(rank, 2)

    def z_of(r):
        return lax.rem(r + 2 * ic, 4)

    def turn(i, by):
        return lax.rem(i + by, 4)

    loads = [
        pltpu.make_async_copy(wq, wqs, lsem.at[0]),
        pltpu.make_async_copy(wv, wvs, lsem.at[1]),
        pltpu.make_async_copy(wk, wks, lsem.at[2]),
    ]
    for c in loads:
        c.start()
    late = [pltpu.make_async_copy(w_inner, wi, lsem.at[3]), pltpu.make_async_copy(w_outer, wt, lsem.at[4])]
    for k in range(G):
        at = pl.multiple_of(turn(iz, k) * 192, 192)
        late.append(pltpu.make_async_copy(w_out.at[pl.ds(at, 192)], wo.at[pl.ds(192 * k, 192)], lsem.at[5 + k]))

    barrier = pltpu.get_barrier_semaphore()
    peers = [{"dp_2": 1 - ic}]
    for i in (1, 2, 3):
        peers += [{"heads": turn(iz, i)}, {"dp_0": turn(ix, i)}, {"dp_1": turn(iy, i)}]
    for where in peers:
        pl.semaphore_signal(barrier, inc=1, device_id=where, device_id_type=MESH)
    pl.semaphore_wait(barrier, 10)

    def slot(ref, r):
        return ref.at[pl.ds(pl.multiple_of(r * Q, Q), Q)]

    def spread(src, dst, sem):
        for j in range(B):
            @pl.when(rank != j)
            def _():
                remote(src.at[j], slot(dst, rank), sem.at[0, j], sem.at[1, rank], heads=z_of(j)).start()

            @pl.when(rank == j)
            def _():
                pltpu.make_async_copy(src.at[j], slot(dst, rank), sem.at[1, j]).start()

    def spread_wait(src, dst, sem):
        @pl.when(owner)
        def _():
            for r in range(4):
                pltpu.make_async_copy(src.at[0], dst.at[pl.ds(r * Q, Q)], sem.at[1, r]).wait()

    def spread_end(src, dst, sem):
        for j in range(B):
            @pl.when(rank != j)
            def _():
                remote(src.at[j], slot(dst, rank), sem.at[0, j], sem.at[1, rank], heads=z_of(j)).wait_send()

    spread(inputs, x, xsem)

    for c in loads:
        c.wait()
    wg[0] = jnp.concatenate(
        [wqs[...], wvs[...], wks[...], dq[...], dv[...], jnp.zeros((D, GW - 592), BF)], axis=1
    )
    up[:, 0:64, :] = jnp.zeros((G, 64, 384), BF)
    up[:, 80:128, :] = jnp.zeros((G, 48, 384), BF)
    zero8 = jnp.zeros((8, 192), F32)
    both = jnp.concatenate(
        [
            jnp.concatenate([uq[...].astype(F32), zero8], axis=1),
            jnp.concatenate([zero8, uv[...].astype(F32)], axis=1),
        ],
        axis=0,
    )
    up[0, 64:80, :] = (2.0 * both).astype(BF)
    rows0 = jnp.where(ic == 0, 192 * iy + 48 * ix, 192 * ix + 48 * iy)
    rows0 = pl.multiple_of(rows0, 48)

    def part(c, k, at, count):
        return wg.at[k, pl.ds(at, count), pl.ds(*LANES[c])]

    def over_z(c):
        return [
            remote(part(c, 0, rows0, 48), part(c, 4 - i, rows0, 48), wsem.at[0, i], wsem.at[1, 4 - i],
                   heads=turn(iz, i))
            for i in (1, 2, 3)
        ]

    def first(c):
        axis, me = (("dp_0", ix), ("dp_1", iy))[c]
        block = wg.at[pl.ds(1, 3), pl.ds(rows0, 48), pl.ds(*LANES[c])]
        return [remote(block, block, w1.at[0, i], w1.at[1, i], **{axis: turn(me, i)}) for i in (1, 2, 3)]

    def second(c, k):
        axis, me, line = (("dp_1", iy, iy), ("dp_0", ix, ix))[c]
        block = part(c, k, pl.multiple_of(192 * line, 192), 192)
        return [remote(block, block, w2.at[0, k, i], w2.at[1, k, i], **{axis: turn(me, i)}) for i in (1, 2, 3)]

    def third(c, k):
        block = part(c, k, 0, D)
        return remote(block, block, w3.at[0, k], w3.at[1, k], dp_2=1 - ic)

    def each_core(do):
        for c in (0, 1):
            @pl.when(ic == c)
            def _():
                do(c)

    ups = [
        remote(up.at[0, pl.ds(64, 16)], up.at[4 - i, pl.ds(64, 16)], usem.at[0, i], usem.at[1, 4 - i], heads=turn(iz, i))
        for i in (1, 2, 3)
    ]
    for c in ups:
        c.start()
    each_core(lambda c: [d.start() for d in over_z(c)])
    for c in late:
        c.start()
    each_core(lambda c: [d.wait_recv() for d in over_z(c)])
    each_core(lambda c: [d.start() for d in first(c)])
    spread(cot, ct, csem)
    each_core(lambda c: [d.wait_recv() for d in first(c)])
    each_core(lambda c: [d.start() for k in (1, 2, 3) for d in second(c, k)])
    for c in ups:
        c.wait_recv()

    row = jnp.where(mine == 0, kmask[0:1], jnp.where(mine == 1, kmask[1:2], kmask[2:3]))
    row = jnp.where(ic == 0, row, jnp.concatenate([row[:, 256:512], row[:, 0:256]], axis=1))
    row = jnp.where(row > 0, 0.0, -1e30).astype(F32)
    bias[...] = jnp.broadcast_to(row, (128, S)).T[:, 0:1]
    spread_wait(inputs, x, xsem)

    def fwd(k, _):
        @pl.when(k > 0)
        def _():
            def do(c):
                third(1 - c, k).wait_recv()
            each_core(do)

        @pl.when(owner)
        def _():
            project(k, x, wg, up, bias, knat, vnat, yt)

        @pl.when(k < 3)
        def _():
            def do(c):
                for d in second(c, k + 1):
                    d.wait_recv()
                third(c, k + 1).start()
            each_core(do)

        @pl.when(owner)
        def _():
            attend(k, knat, yt, sscr, p, rl, ctxt)

        return 0

    lax.fori_loop(0, G, fwd, 0)
    for c in late:
        c.wait()

    @pl.when(owner)
    def _():
        ctx = jnp.concatenate([ctxt[g].T for g in range(G)], axis=1)
        h1 = x[...].astype(F32) + nn(ctx, wo[...])
        xh, r = norm(h1)
        xhat1[...] = xh
        r1s[:, 0:1] = r
        n1v = xh * g1[...] + b1[...]
        n1b[...] = n1v.astype(BF)
        acc[...] = n1v

        def ffn(c, _):
            cols = pl.ds(pl.multiple_of(c * 2 * C, 2 * C), 2 * C)
            h = nn(n1b[...], wi[:, cols])
            a, da = gelu_pair(h)
            dact[:, cols] = da
            acc[...] += nn(a.astype(BF), wt[cols, :])
            return 0

        lax.fori_loop(0, FF // (2 * C), ffn, 0)
        xh2, r2 = norm(acc[...])
        act[...] = (xh2 * g2[...] + b2[...]).astype(BF)
        acc[...] = xh2
        r1s[:, 1:2] = r2

    def back(src, dst, sem):
        @pl.when(owner)
        def _():
            for t in range(4):
                @pl.when(rank != t)
                def _():
                    remote(src.at[pl.ds(t * Q, Q)], dst.at[mine], sem.at[0, t], sem.at[1, mine], heads=z_of(t)).start()

                @pl.when(rank == t)
                def _():
                    pltpu.make_async_copy(src.at[pl.ds(t * Q, Q)], dst.at[mine], sem.at[1, mine]).start()

    def back_end(src, dst, sem):
        for j in range(B):
            pltpu.make_async_copy(src.at[pl.ds(0, Q)], dst.at[j], sem.at[1, j]).wait()

        @pl.when(owner)
        def _():
            for t in range(4):
                @pl.when(rank != t)
                def _():
                    remote(src.at[pl.ds(t * Q, Q)], dst.at[mine], sem.at[0, t], sem.at[1, mine], heads=z_of(t)).wait_send()

    back(act, act_out, asem)
    spread_wait(cot, ct, csem)

    @pl.when(owner)
    def _():
        limit = lengths[mine]
        at = lax.broadcasted_iota(jnp.int32, (Q, 1), 0)
        valid = jnp.concatenate([at + z_of(t) * Q < limit for t in range(4)], axis=0)
        tangent = jnp.where(valid, ct[...].astype(F32), 0.0)
        gs = norm_back(tangent * g2[...], acc[...], r1s[:, 1:2])
        gnb[...] = gs.astype(BF)
        acc[...] = gs

        def ffn_back(c, _):
            cols = pl.ds(pl.multiple_of(c * 2 * C, 2 * C), 2 * C)
            ga = nt(gnb[...], wt[cols, :])
            gi = (ga * dact[:, cols]).astype(BF)
            acc[...] += nt(gi, wi[:, cols])
            return 0

        lax.fori_loop(0, FF // (2 * C), ffn_back, 0)
        gf1 = norm_back(acc[...] * g1[...], xhat1[...], r1s[:, 0:1])
        acc[...] = gf1
        gfb = gf1.astype(BF)
        for g in range(G):
            dot_ref[g] = nt(wo[192 * g : 192 * g + 192, :], gfb)

        def bwd(g, gm):
            attend_back(g, vnat, yt, p, rl, ctxt, dot_ref, dsscr, dyt)
            mid = yt[g, 576:592, :]
            first_rows = lax.broadcasted_iota(jnp.int32, (16, 192), 0) < 8
            gu = jnp.where(first_rows, nt(mid, dyt[g, 0:192, :]), nt(mid, dyt[g, 192:384, :]))
            msg[g, 0:16, 0:192] = gu * 2.0
            return gm + nn(up[g, 64:80, :], dyt[g, 0:384, :])

        gmb = lax.fori_loop(0, G, bwd, jnp.zeros((16, S), F32)).astype(BF)
        gd = nn(gmb, x[...])
        for q in range(4):
            gdp[q, :, 0:192] = gd[:, 192 * q : 192 * q + 192]
        for k in range(G):
            msg[k, 16:32, 0:192] = gdp[turn(iz, k), :, 0:192]
            dyt[k, 576:GW, :] = jnp.concatenate(
                [gmb if k == 0 else jnp.zeros((16, S), BF), jnp.zeros((48, S), BF)], axis=0
            )

    zsum = [remote(msg.at[i], redz.at[4 - i], gz.at[0, i], gz.at[1, 4 - i], heads=turn(iz, i)) for i in (1, 2, 3)]

    @pl.when(owner)
    def _():
        for c in zsum:
            c.start()

    @pl.when(owner)
    def _():
        total = acc[...]
        for g in range(G):
            total = total + nt(dyt[g].T, wg[g])
        igb[...] = total.astype(BF)

    back(igb, ig_out, isem)

    @pl.when(owner)
    def _():
        redz[0] = msg[0]

    @pl.when(rank == 3)
    def _():
        redz[0] = jnp.zeros((32, 256), F32)

    for i in (1, 2, 3):
        from_owner = turn(rank, i) != 3

        @pl.when(from_owner)
        def _():
            pltpu.make_async_copy(msg.at[i], redz.at[i], gz.at[1, i]).wait()
            redz[0] += redz[i]

    step = remote(redz.at[0], redc, gc.at[0], gc.at[1], dp_2=1 - ic)
    step.start()
    step.wait()

    def line(value, buf, sem, axis, me):
        buf[me] = value
        copies = [remote(buf.at[me], buf.at[me], sem.at[0, i], sem.at[1, i], **{axis: turn(me, i)}) for i in (1, 2, 3)]
        for c in copies:
            c.start()
        for c in copies:
            c.wait()
        return buf[0] + buf[1] + buf[2] + buf[3]

    total = line(redz[0] + redc[...], redx, gx, "dp_0", ix)
    total = line(total, redy, gy, "dp_1", iy)
    gu_out[...] = total[0:16]
    gd_out[iz] = total[16:32]
    copies = [
        remote(gd_out.at[iz], gd_out.at[iz], gf.at[0, i], gf.at[1, i], heads=turn(iz, i)) for i in (1, 2, 3)
    ]
    for c in copies:
        c.start()
    for c in copies:
        c.wait()

    back_end(act, act_out, asem)
    back_end(igb, ig_out, isem)
    spread_end(inputs, x, xsem)
    spread_end(cot, ct, csem)
    for c in ups:
        c.wait_send()
    each_core(lambda c: [d.wait_send() for d in over_z(c) + first(c)])
    each_core(lambda c: [d.wait_send() for k in (1, 2, 3) for d in second(c, k) + [third(c, k)]])

    @pl.when(owner)
    def _():
        for c in zsum:
            c.wait_send()


def finish(act_in, ig_in, gd, gu, act, ig, gdq, guq, gdv, guv):
    act[...] = act_in[...]
    ig[...] = ig_in[...].astype(F32)

    @pl.when(pl.program_id(0) == 0)
    def _():
        cols = jnp.concatenate([gd[q, :, 0:192] for q in range(4)], axis=1).T
        gdq[...] = cols[:, 0:8]
        gdv[...] = cols[:, 8:16]
        guq[...] = gu[0:8, 0:192]
        guv[...] = gu[8:16, 0:192]


def scratch():
    V, dma = pltpu.VMEM, pltpu.SemaphoreType.DMA
    return [
        V((S, D), BF), V((S, D), BF), V((D, 192), BF), V((D, 192), BF), V((D, 192), BF),
        V((D, D), BF), V((D, FF), BF), V((FF, D), BF), V((G, D, GW), BF), V((G, 128, 384), BF),
        V((S, D), BF), V((S, D), BF),
        V((S, 1), F32), V((G, S, 256), BF), V((G, S, 256), BF), V((G, GW, S), BF),
        V((3, 2, S, 256), F32), V((12, S, S), BF), V((12, 1, S), F32), V((G, 192, S), BF),
        V((S, D), F32), V((S, 2), F32), V((S, D), BF),
        V((S, FF), F32), V((S, D), F32), V((G, 192, S), F32), V((3, S, S), BF), V((G, GW, S), BF), V((S, D), BF),
        V((4, 32, 256), F32), V((4, 32, 256), F32), V((32, 256), F32), V((4, 32, 256), F32), V((4, 32, 256), F32),
        V((4, 16, 256), F32),
        dma((9,)), dma((2, 4)), dma((2, 4)), dma((2, 4)), dma((2, 4)), dma((2, 4)), dma((2, 4, 4)), dma((2, 4)),
        dma((2, 4)), dma((2, 4)), dma((2, 4)), dma((2,)), dma((2, 4)), dma((2, 4)), dma((2, 4)),
    ]


def per_device(inputs, key_mask, lengths, cotangent, wq, wk, wv, w_out, w_inner, w_outer, g1, b1, g2, b2, dq, uq, dv, uv):
    vm, hbm = pl.BlockSpec(memory_space=pltpu.VMEM), pl.BlockSpec(memory_space=pl.ANY)
    shape = jax.ShapeDtypeStruct
    act, ig, gd, gu = pl.pallas_call(
        layer,
        out_shape=(shape((B, Q, D), BF), shape((B, Q, D), BF), shape((4, 16, 256), F32), shape((16, 256), F32)),
        in_specs=[hbm, hbm, vm, pl.BlockSpec(memory_space=pltpu.SMEM)] + [hbm] * 6 + [vm] * 8,
        out_specs=(hbm, hbm, vm, vm),
        scratch_shapes=scratch(),
        compiler_params=pltpu.CompilerParams(
            collective_id=0, has_side_effects=True, vmem_limit_bytes=62 * 2**20
        ),
    )(
        inputs, cotangent, key_mask, lengths, wq, wk, wv, w_out, w_inner, w_outer,
        g1[None], b1[None], g2[None], b2[None], dq, uq, dv, uv,
    )
    one = pl.BlockSpec((1, Q, D), lambda j: (j, 0, 0))

    def whole(*dims):
        return pl.BlockSpec(dims, lambda j: (0,) * len(dims))

    act, ig, gdq, guq, gdv, guv = pl.pallas_call(
        finish,
        grid=(B,),
        out_shape=(
            shape((B, Q, D), BF), shape((B, Q, D), F32),
            shape((D, 8), F32), shape((8, 192), F32), shape((D, 8), F32), shape((8, 192), F32),
        ),
        in_specs=[one, one, whole(4, 16, 256), whole(16, 256)],
        out_specs=(one, one, whole(D, 8), whole(8, 192), whole(D, 8), whole(8, 192)),
    )(act, ig, gd, gu)
    return act, ig, gdq, guq, gdv, guv


def solution(mesh):
    finer = Mesh(
        mesh.devices.reshape(4, 4, 2, mesh.shape["heads"]), ("dp_0", "dp_1", "dp_2", "heads")
    )
    rows, cols, same = P(DP, "heads", None), P(None, "heads"), P()
    return jax.shard_map(
        per_device,
        mesh=finer,
        in_specs=(rows, P(DP, None), P(DP), rows, cols, cols, cols) + (same,) * 8 + (cols, same, cols),
        out_specs=(rows, rows, same, cols, same, cols),
        check_vma=False,
    )
```

time: 285 us -> 118 us (0.41)
  Pallas kernels: 0 us -> 99.6 us
  waiting for transfers between devices: 70 us -> 0 us
  blocking collectives: 67.6 us -> 0 us
  matrix products: 66.4 us -> 0 us
  starting transfers between devices: 21.7 us -> 0 us
  other arithmetic: 20.2 us -> 0 us
  local copies, waits for them, and re-layouts: 36.4 us -> 17.2 us
    pallas_call x0 -> x2, Pallas kernels: none -> 99.6 us  [the longest x1 95.6 us: per_device(): pl.pallas_call(layer, out_shape=(shape((B, Q, D), BF), shape((B, Q, D), B...]
    all_to_all x4 -> x0, waiting for transfers between devices: 70 us -> none  [the longest x2 29.5 us: sent_to_all(): return lax.all_to_all(copies, axis, split_axis=0, concat_axis=0, tiled=True)]
    dot_general x44 -> x0, matrix products: 66.4 us -> none  [the longest x1 13.2 us: per_device(): jnp.dot(normed_one.astype(jnp.bfloat16), w_inner, preferred_element_type=...]
    psum x4 -> x0, blocking collectives: 54.8 us -> none  [by_axis(): return functools.reduce(lax.psum, axes, value)]
    all_to_all x4 -> x0, starting transfers between devices: 21.7 us -> none  [the longest x2 12.7 us: sent_to_all(): return lax.all_to_all(copies, axis, split_axis=0, concat_axis=0, tiled=True)]
    all_to_all x1 -> x0, blocking collectives: 12.8 us -> none  [per_device(): lax.all_to_all(grad_context, 'heads', split_axis=2, concat_axis=1, tiled=...]
    reduce_sum x9 -> x0, other arithmetic: 8.6 us -> none  [the longest x2 3.43 us: layer_norm(): center = hidden - jnp.mean(hidden, axis=-1, keepdims=True)]
    reshape x10 -> x0, local copies, waits for them, and re-layouts: 5.78 us -> none  [the longest x1 2.64 us: per_device(): own_flat = context_own.reshape(seq_count * own_rows, features)]
  transfers between devices with their start and end apart: 4 -> 0, of which waited for: 3 -> 0; matrix products, arithmetic and copies ran while one was open for 6% -> 0% of each run, Pallas kernels for 0% -> 0%
where the time goes in v1:
time: 118 us; the launch traced here: 117 us
  Pallas kernels  99.6 us (84%)
  local copies, waits for them, and re-layouts  17.2 us (15%)
    pallas_call x1, Pallas kernels, per_device(): pl.pallas_call(layer, out_shape=(shape((B, Q, D), BF), shape((B, Q, D), B...  95.6 us
    unnamed x5, local copies, waits for them, and re-layouts  8.68 us
    pallas_call x1, Pallas kernels, per_device(): pl.pallas_call(finish, grid=(B,), out_shape=(shape((B, Q, D), BF), shape(...  3.99 us
    pallas_call x2, local copies, waits for them, and re-layouts, per_device(): pl.pallas_call(finish, grid=(B,), out_shape=(shape((B, Q, D), BF), shape(...  3.48 us

profile of v1, /device:TPU:0, one launch (start us, length us, event | category | flops | bytes accessed | tf_op | source)
XLA Modules:
  0.0 117.5 jit_solution(10404432805820770528)
XLA Ops:
  0.6 1.3 %broadcast_in_dim.12.g1 = f32[1,768]{1,0:T(1,128)} reshape(f32[768]{0:T(1024)} %param.28) | data formatting | bytes 6144 | tf_op jit(solution)/shard_map/broadcast_in_dim | solution.py:494
  1.9 1.3 %broadcast_in_dim.13.b1 = f32[1,768]{1,0:T(1,128)} reshape(f32[768]{0:T(1024)} %param.29) | data formatting | bytes 6144 | tf_op jit(solution)/shard_map/broadcast_in_dim | solution.py:494
  3.2 1.3 %broadcast_in_dim.14.g2 = f32[1,768]{1,0:T(1,128)} reshape(f32[768]{0:T(1024)} %param.30) | data formatting | bytes 6144 | tf_op jit(solution)/shard_map/broadcast_in_dim | solution.py:494
  4.4 1.3 %broadcast_in_dim.15.b2 = f32[1,768]{1,0:T(1,128)} reshape(f32[768]{0:T(1024)} %param.31) | data formatting | bytes 6144 | tf_op jit(solution)/shard_map/broadcast_in_dim | solution.py:494
  5.7 1.5 %copy.27.dq = bf16[768,8]{1,0:T(8,128)(2,1)} copy(bf16[768,8]{0,1:T(8,128)(2,1)} %param.32) | data formatting | bytes 24576 | tf_op args[14]
  7.2 1.5 %copy.28.dv = bf16[768,8]{1,0:T(8,128)(2,1)} copy(bf16[768,8]{0,1:T(8,128)(2,1)} %param.34) | data formatting | bytes 24576 | tf_op args[16]
  8.7 1.9 %copy.24.wq = bf16[768,192]{1,0:T(8,128)(2,1)} copy(bf16[768,192]{0,1:T(8,128)(2,1)} %param.22) | data formatting | bytes 589824 | tf_op args[4]
  10.6 1.9 %copy.25.wk = bf16[768,192]{1,0:T(8,128)(2,1)} copy(bf16[768,192]{0,1:T(8,128)(2,1)} %param.23) | data formatting | bytes 589824 | tf_op args[5]
  12.5 1.9 %copy.26.wv = bf16[768,192]{1,0:T(8,128)(2,1)} copy(bf16[768,192]{0,1:T(8,128)(2,1)} %param.24) | data formatting | bytes 589824 | tf_op args[6]
  14.4 95.6 %shard_map.217 = (bf16[3,128,768]{2,1,0:T(8,128)(2,1)}, bf16[3,128,768]{2,1,0:T(8,128)(2,1)}, f32[4,16,256]{2,1,0:T(8,128)}, f32[16,256]{1,0:T(8,128)}) custom-call(bf16[3,128,768]{2,1,0:T(8,128)(2,1)} %inputs.1, bf16[3,128,768]{2,1,0:T(8,128)(2,1)} %cot.1, s32[3,512]{1,0:T(4,128)} %kmask.1, s32[3]{0:T(128)} %lengths.1, bf16[768,192]{1,0:T(8,128)(2,1)} %copy.24.wq, ...), custom_call_target="tpu_custom_call" | custom-call | tf_op jit(solution)/shard_map/pallas_call | solution.py:483
  110.0 4.0 %shard_map.218 = (bf16[3,128,768]{2,1,0:T(8,128)(2,1)}, f32[3,128,768]{2,1,0:T(8,128)}, f32[768,8]{1,0:T(8,128)}, f32[8,192]{1,0:T(8,128)}, f32[768,8]{1,0:T(8,128)}, /*index=5*/f32[8,192]{1,0:T(8,128)}) custom-call(bf16[3,128,768]{2,1,0:T(8,128)(2,1)} %get-tuple-element.10.act_in, bf16[3,128,768]{2,1,0:T(8,128)(2,1)} %get-tuple-element.11.ig_in, ...), custom_call_target="tpu_custom_call" | custom-call | tf_op jit(solution)/shard_map/pallas_call | solution.py:501
  114.0 1.7 %copy.29 = f32[768,8]{0,1:T(8,128)} copy(f32[768,8]{1,0:T(8,128)} %get-tuple-element.16) | data formatting | bytes 49152 | tf_op jit(solution)/shard_map/pallas_call | solution.py:501
  115.7 1.7 %copy.30 = f32[768,8]{0,1:T(8,128)} copy(f32[768,8]{1,0:T(8,128)} %get-tuple-element.18) | data formatting | bytes 49152 | tf_op jit(solution)/shard_map/pallas_call | solution.py:501

commit v2 on v1

--- a/solution.py
+++ b/solution.py
@@ -12,11 +12,10 @@
 S, D, FF, HD, G = 512, 768, 3072, 64, 4
 B, Q = 3, 128
 GW = 640
-C = 256
+C = 512
 NT = (((1,), (1,)), ((), ()))
 DP = ("dp_0", "dp_1", "dp_2")
 MESH = pl.DeviceIdType.MESH
-LANES = ((0, 384), (384, 256))
 
 
 def nn(a, b):
@@ -27,19 +26,24 @@
     return lax.dot_general(a, b, NT, preferred_element_type=F32)
 
 
-def project(g, x, wg, up, bias, knat, vnat, yt):
+def middle(x, down, mid):
+    mid[0:16, :] = nt(down[...], x[...]).astype(BF)
+    mid[16:64, :] = jnp.zeros((48, S), BF)
+
+
+def project(g, x, wg, up, mid, bias, knat, vnat, yt):
     xv = x[...]
-    tail = nn(xv, wg[g, :, 384:GW])
-    lane = lax.broadcasted_iota(jnp.int32, (S, 256), 1)
-    kb = jnp.where(lane == 255, bias[...], tail).astype(BF)
-    knat[g] = kb
-    qv = nn(xv, wg[g, :, 0:384]) + nn(kb[:, 128:256], up[g])
-    lane2 = lax.broadcasted_iota(jnp.int32, (S, 384), 1)
-    qvb = qv.astype(BF)
-    vnat[g] = qvb[:, 128:384]
-    qvs = jnp.where(lane2 < 192, qvb * 0.125, qvb).astype(BF)
-    yt[g, 0:384, :] = qvs.T
-    yt[g, 384:GW, :] = kb.T
+    at = pl.multiple_of(g * 576, 576)
+    upt = jnp.concatenate([up[g], jnp.zeros((112, 384), BF)], axis=0).T
+    middle_rows = jnp.concatenate([mid[...], jnp.zeros((64, S), BF)], axis=0)
+    kt = jnp.concatenate([nt(wg[pl.ds(at + 384, 192), :], xv).astype(BF), bias[...]], axis=0)
+    yt[g, 384:GW, :] = kt
+    knat[g] = kt.T
+    qv = nt(wg[pl.ds(at, 384), :], xv) + nn(upt, middle_rows)
+    vt = qv[192:384].astype(BF)
+    yt[g, 0:192, :] = (qv[0:192].astype(BF).astype(F32) * 0.125).astype(BF)
+    yt[g, 192:384, :] = vt
+    vnat[g] = jnp.concatenate([jnp.zeros((64, S), BF), vt], axis=0).T
 
 
 def pad_rows(piece, before, total):
@@ -74,6 +78,7 @@
 
 def attend_back(g, vnat, yt, p, rl, ctxt, dot_ref, dsscr, dyt):
     vb = vnat[g]
+    at = pl.multiple_of(g * 576, 576)
     for j in range(3):
         h = g * 3 + j
         rows = slice(64 * j, 64 * j + 64)
@@ -84,10 +89,10 @@
             cols = slice(256 * half, 256 * half + 256)
             dp = nn(vb, rhs[:, cols])
             dsscr[j, :, cols] = (p[h, :, cols].astype(F32) * (dp - dsum[:, cols])).astype(BF)
-        dyt[g, 192 + 64 * j : 256 + 64 * j, :] = nt(do, p[h]).astype(BF)
+        dyt[pl.ds(at + 192 + 64 * j, 64), :] = nt(do, p[h]).astype(BF)
         ds = dsscr[j]
-        dyt[g, 384 + 64 * j : 448 + 64 * j, :] = nt(yt[g, rows, :], ds).astype(BF)
-        dyt[g, rows, :] = (nn(yt[g, 384 + 64 * j : 448 + 64 * j, :], ds) * 0.125).astype(BF)
+        dyt[pl.ds(at + 384 + 64 * j, 64), :] = nt(yt[g, rows, :], ds).astype(BF)
+        dyt[pl.ds(at + 64 * j, 64), :] = (nn(yt[g, 384 + 64 * j : 448 + 64 * j, :], ds) * 0.125).astype(BF)
 
 
 def gelu_pair(v):
@@ -109,6 +114,54 @@
     return r * (n - jnp.mean(n, axis=-1, keepdims=True) - xhat * jnp.mean(n * xhat, axis=-1, keepdims=True))
 
 
+def chunk(c):
+    return pl.ds(pl.multiple_of(c * C, C), C)
+
+
+def feed_forward(n1b, wi, wt, ha, hb, aa, ab, dact, acc):
+    last = FF // C - 1
+
+    def act(h, a, c):
+        v, d = gelu_pair(h[...])
+        a[...] = v.astype(BF)
+        dact[:, chunk(c)] = d.astype(dact.dtype)
+
+    ha[...] = nn(n1b[...], wi[:, chunk(0)])
+
+    def pair(i, _):
+        c = 2 * i
+        hb[...] = nn(n1b[...], wi[:, chunk(c + 1)])
+        act(ha, aa, c)
+        ha[...] = nn(n1b[...], wi[:, chunk(jnp.minimum(c + 2, last))])
+        acc[...] += nn(aa[...], wt[chunk(c), :])
+        act(hb, ab, c + 1)
+        acc[...] += nn(ab[...], wt[chunk(c + 1), :])
+        return 0
+
+    lax.fori_loop(0, FF // C // 2, pair, 0)
+
+
+def feed_back(gnb, wi, wt, ga, aa, ab, dact, acc):
+    last = FF // C - 1
+
+    def grad(c):
+        return nt(gnb[...], wt[chunk(c), :])
+
+    def through(h, a, c):
+        a[...] = (h * dact[:, chunk(c)].astype(F32)).astype(BF)
+
+    through(grad(0), aa, 0)
+
+    def pair(i, _):
+        c = 2 * i
+        through(grad(c + 1), ab, c + 1)
+        acc[...] += nt(aa[...], wi[:, chunk(c)])
+        n = jnp.minimum(c + 2, last)
+        through(grad(n), aa, n)
+        acc[...] += nt(ab[...], wi[:, chunk(c + 1)])
+        return 0
+
+    lax.fori_loop(0, FF // C // 2, pair, 0)
 def remote(src, dst, send, recv, **where):
     return pltpu.make_async_remote_copy(
         src_ref=src, dst_ref=dst, send_sem=send, recv_sem=recv, device_id=where, device_id_type=MESH
@@ -118,9 +171,9 @@
 def layer(
     inputs, cot, kmask, lengths, wq, wk, wv, w_out, w_inner, w_outer, g1, b1, g2, b2, dq, uq, dv, uv,
     act_out, ig_out, gd_out, gu_out,
-    x, ct, wqs, wks, wvs, wo, wi, wt, wg, up, act, igb,
-    bias, knat, vnat, yt, sscr, p, rl, ctxt, xhat1, r1s, n1b, dact, acc, dot_ref, dsscr, dyt, gnb,
-    msg, redz, redc, redx, redy, gdp,
+    x, ct, wo, wi, wt, wg, up, down, act, igb,
+    bias, mid, knat, vnat, yt, sscr, p, rl, ctxt, xhat1, r1s, n1b, ha, hb, aa, ab, dact, acc, dot_ref, dsscr, dyt, gnb,
+    msg, redz, redc, redx, redy, gdp, gmid,
     lsem, xsem, csem, wsem, usem, w1, w2, w3, asem, isem, gz, gc, gx, gy, gf,
 ):
     ix, iy, ic, iz = (lax.axis_index(a) for a in ("dp_0", "dp_1", "dp_2", "heads"))
@@ -135,9 +188,7 @@
         return lax.rem(i + by, 4)
 
     loads = [
-        pltpu.make_async_copy(wq, wqs, lsem.at[0]),
-        pltpu.make_async_copy(wv, wvs, lsem.at[1]),
-        pltpu.make_async_copy(wk, wks, lsem.at[2]),
+        pltpu.make_async_copy(w, wg.at[pl.ds(192 * n, 192)], lsem.at[n]) for n, w in enumerate((wq, wv, wk))
     ]
     for c in loads:
         c.start()
@@ -183,11 +234,7 @@
 
     for c in loads:
         c.wait()
-    wg[0] = jnp.concatenate(
-        [wqs[...], wvs[...], wks[...], dq[...], dv[...], jnp.zeros((D, GW - 592), BF)], axis=1
-    )
-    up[:, 0:64, :] = jnp.zeros((G, 64, 384), BF)
-    up[:, 80:128, :] = jnp.zeros((G, 48, 384), BF)
+    down[...] = jnp.concatenate([dq[...].astype(F32), dv[...].astype(F32)], axis=0).astype(BF)
     zero8 = jnp.zeros((8, 192), F32)
     both = jnp.concatenate(
         [
@@ -196,62 +243,82 @@
         ],
         axis=0,
     )
-    up[0, 64:80, :] = (2.0 * both).astype(BF)
-    rows0 = jnp.where(ic == 0, 192 * iy + 48 * ix, 192 * ix + 48 * iy)
-    rows0 = pl.multiple_of(rows0, 48)
+    up[0] = (2.0 * both).astype(BF)
+    row_of = ((iy, ix), (ix, iy))
 
     def part(c, k, at, count):
-        return wg.at[k, pl.ds(at, count), pl.ds(*LANES[c])]
+        return wg.at[pl.ds(pl.multiple_of(576 * k + at, 16), count), pl.ds(384 * c, 384)]
 
     def over_z(c):
+        b, a = row_of[c]
         return [
-            remote(part(c, 0, rows0, 48), part(c, 4 - i, rows0, 48), wsem.at[0, i], wsem.at[1, 4 - i],
-                   heads=turn(iz, i))
+            remote(part(c, 0, 192 * b + 48 * a, 48), part(c, 4 - i, 192 * b + 48 * a, 48), wsem.at[0, i],
+                   wsem.at[1, 4 - i], heads=turn(iz, i))
             for i in (1, 2, 3)
         ]
 
     def first(c):
-        axis, me = (("dp_0", ix), ("dp_1", iy))[c]
-        block = wg.at[pl.ds(1, 3), pl.ds(rows0, 48), pl.ds(*LANES[c])]
-        return [remote(block, block, w1.at[0, i], w1.at[1, i], **{axis: turn(me, i)}) for i in (1, 2, 3)]
-
-    def second(c, k):
-        axis, me, line = (("dp_1", iy, iy), ("dp_0", ix, ix))[c]
-        block = part(c, k, pl.multiple_of(192 * line, 192), 192)
-        return [remote(block, block, w2.at[0, k, i], w2.at[1, k, i], **{axis: turn(me, i)}) for i in (1, 2, 3)]
+        b, a = row_of[c]
+        axis = ("dp_0", "dp_1")[c]
+        blocks = [part(c, k, 192 * b + 48 * a, 48) for k in (0, 1, 2, 3)]
+        return [
+            remote(blocks[k], blocks[k], w1.at[0, k, i], w1.at[1, k, i], **{axis: turn(a, i)})
+            for k in (1, 2, 3) for i in (1, 2, 3)
+        ]
+
+    def second(c, k, i, back):
+        b, a = row_of[c]
+        axis = ("dp_1", "dp_0")[c]
+        block = part(c, k, 192 * (turn(b, 4 - i) if back else b), 192)
+        return remote(block, block, w2.at[0, k, i], w2.at[1, k, i], **{axis: turn(b, i)})
+
+    def holds(c):
+        return row_of[c][0] < 3
+
+    def second_start(c, k):
+        for i in (1, 2, 3):
+            second(c, k, i, False).start()
+
+    def second_recv(c, k):
+        for i in (1, 2, 3):
+            @pl.when(turn(row_of[c][0], 4 - i) < 3)
+            def _():
+                second(c, k, i, True).wait_recv()
 
     def third(c, k):
-        block = part(c, k, 0, D)
+        block = part(c, k, 0, 576)
         return remote(block, block, w3.at[0, k], w3.at[1, k], dp_2=1 - ic)
 
-    def each_core(do):
+    def each_core(do, only=lambda c: True):
         for c in (0, 1):
-            @pl.when(ic == c)
+            @pl.when(jnp.logical_and(ic == c, only(c)))
             def _():
                 do(c)
 
     ups = [
-        remote(up.at[0, pl.ds(64, 16)], up.at[4 - i, pl.ds(64, 16)], usem.at[0, i], usem.at[1, 4 - i], heads=turn(iz, i))
+        remote(up.at[0], up.at[4 - i], usem.at[0, i], usem.at[1, 4 - i], heads=turn(iz, i))
         for i in (1, 2, 3)
     ]
     for c in ups:
         c.start()
-    each_core(lambda c: [d.start() for d in over_z(c)])
+    each_core(lambda c: [d.start() for d in over_z(c)], holds)
     for c in late:
         c.start()
-    each_core(lambda c: [d.wait_recv() for d in over_z(c)])
-    each_core(lambda c: [d.start() for d in first(c)])
+    each_core(lambda c: [d.wait_recv() for d in over_z(c)], holds)
+    each_core(lambda c: [d.start() for d in first(c)], holds)
     spread(cot, ct, csem)
-    each_core(lambda c: [d.wait_recv() for d in first(c)])
-    each_core(lambda c: [d.start() for k in (1, 2, 3) for d in second(c, k)])
+    for k in (1, 2, 3):
+        each_core(lambda c: [d.wait_recv() for d in first(c)[3 * k - 3 : 3 * k]], holds)
+        each_core(lambda c: second_start(c, k), holds)
     for c in ups:
         c.wait_recv()
 
     row = jnp.where(mine == 0, kmask[0:1], jnp.where(mine == 1, kmask[1:2], kmask[2:3]))
     row = jnp.where(ic == 0, row, jnp.concatenate([row[:, 256:512], row[:, 0:256]], axis=1))
     row = jnp.where(row > 0, 0.0, -1e30).astype(F32)
-    bias[...] = jnp.broadcast_to(row, (128, S)).T[:, 0:1]
+    bias[...] = jnp.where(lax.broadcasted_iota(jnp.int32, (64, S), 0) == 63, row, 0.0).astype(BF)
     spread_wait(inputs, x, xsem)
+    pl.when(owner)(lambda: middle(x, down, mid))
 
     def fwd(k, _):
         @pl.when(k > 0)
@@ -262,13 +329,12 @@
 
         @pl.when(owner)
         def _():
-            project(k, x, wg, up, bias, knat, vnat, yt)
+            project(k, x, wg, up, mid, bias, knat, vnat, yt)
 
         @pl.when(k < 3)
         def _():
             def do(c):
-                for d in second(c, k + 1):
-                    d.wait_recv()
+                second_recv(c, k + 1)
                 third(c, k + 1).start()
             each_core(do)
 
@@ -289,21 +355,13 @@
         xh, r = norm(h1)
         xhat1[...] = xh
         r1s[:, 0:1] = r
-        n1v = xh * g1[...] + b1[...]
+        n1v = xh * g1[...][None] + b1[...][None]
         n1b[...] = n1v.astype(BF)
         acc[...] = n1v
 
-        def ffn(c, _):
-            cols = pl.ds(pl.multiple_of(c * 2 * C, 2 * C), 2 * C)
-            h = nn(n1b[...], wi[:, cols])
-            a, da = gelu_pair(h)
-            dact[:, cols] = da
-            acc[...] += nn(a.astype(BF), wt[cols, :])
-            return 0
-
-        lax.fori_loop(0, FF // (2 * C), ffn, 0)
+        feed_forward(n1b, wi, wt, ha, hb, aa, ab, dact, acc)
         xh2, r2 = norm(acc[...])
-        act[...] = (xh2 * g2[...] + b2[...]).astype(BF)
+        act[...] = (xh2 * g2[...][None] + b2[...][None]).astype(BF)
         acc[...] = xh2
         r1s[:, 1:2] = r2
 
@@ -339,19 +397,12 @@
         at = lax.broadcasted_iota(jnp.int32, (Q, 1), 0)
         valid = jnp.concatenate([at + z_of(t) * Q < limit for t in range(4)], axis=0)
         tangent = jnp.where(valid, ct[...].astype(F32), 0.0)
-        gs = norm_back(tangent * g2[...], acc[...], r1s[:, 1:2])
+        gs = norm_back(tangent * g2[...][None], acc[...], r1s[:, 1:2])
         gnb[...] = gs.astype(BF)
         acc[...] = gs
 
-        def ffn_back(c, _):
-            cols = pl.ds(pl.multiple_of(c * 2 * C, 2 * C), 2 * C)
-            ga = nt(gnb[...], wt[cols, :])
-            gi = (ga * dact[:, cols]).astype(BF)
-            acc[...] += nt(gi, wi[:, cols])
-            return 0
-
-        lax.fori_loop(0, FF // (2 * C), ffn_back, 0)
-        gf1 = norm_back(acc[...] * g1[...], xhat1[...], r1s[:, 0:1])
+        feed_back(gnb, wi, wt, ha, aa, ab, dact, acc)
+        gf1 = norm_back(acc[...] * g1[...][None], xhat1[...], r1s[:, 0:1])
         acc[...] = gf1
         gfb = gf1.astype(BF)
         for g in range(G):
@@ -359,11 +410,11 @@
 
         def bwd(g, gm):
             attend_back(g, vnat, yt, p, rl, ctxt, dot_ref, dsscr, dyt)
-            mid = yt[g, 576:592, :]
+            at = pl.multiple_of(g * 576, 576)
             first_rows = lax.broadcasted_iota(jnp.int32, (16, 192), 0) < 8
-            gu = jnp.where(first_rows, nt(mid, dyt[g, 0:192, :]), nt(mid, dyt[g, 192:384, :]))
-            msg[g, 0:16, 0:192] = gu * 2.0
-            return gm + nn(up[g, 64:80, :], dyt[g, 0:384, :])
+            gu = nt(mid[0:16, :], dyt[pl.ds(at, 384), :])
+            msg[g, 0:16, 0:192] = jnp.where(first_rows, gu[:, 0:192], gu[:, 192:384]) * 2.0
+            return gm + nn(up[g], dyt[pl.ds(at, 384), :])
 
         gmb = lax.fori_loop(0, G, bwd, jnp.zeros((16, S), F32)).astype(BF)
         gd = nn(gmb, x[...])
@@ -371,9 +422,7 @@
             gdp[q, :, 0:192] = gd[:, 192 * q : 192 * q + 192]
         for k in range(G):
             msg[k, 16:32, 0:192] = gdp[turn(iz, k), :, 0:192]
-            dyt[k, 576:GW, :] = jnp.concatenate(
-                [gmb if k == 0 else jnp.zeros((16, S), BF), jnp.zeros((48, S), BF)], axis=0
-            )
+        gmid[...] = gmb
 
     zsum = [remote(msg.at[i], redz.at[4 - i], gz.at[0, i], gz.at[1, 4 - i], heads=turn(iz, i)) for i in (1, 2, 3)]
 
@@ -384,9 +433,9 @@
 
     @pl.when(owner)
     def _():
-        total = acc[...]
-        for g in range(G):
-            total = total + nt(dyt[g].T, wg[g])
+        gmt = jnp.concatenate([gmid[...], jnp.zeros((112, S), BF)], axis=0).T
+        dn = jnp.concatenate([down[...], jnp.zeros((112, D), BF)], axis=0)
+        total = acc[...] + nn(dyt[...].T, wg[...]) + nn(gmt, dn)
         igb[...] = total.astype(BF)
 
     back(igb, ig_out, isem)
@@ -438,8 +487,9 @@
     spread_end(cot, ct, csem)
     for c in ups:
         c.wait_send()
-    each_core(lambda c: [d.wait_send() for d in over_z(c) + first(c)])
-    each_core(lambda c: [d.wait_send() for k in (1, 2, 3) for d in second(c, k) + [third(c, k)]])
+    each_core(lambda c: [d.wait_send() for d in over_z(c) + first(c)], holds)
+    each_core(lambda c: [second(c, k, i, False).wait_send() for k in (1, 2, 3) for i in (1, 2, 3)], holds)
+    each_core(lambda c: [third(c, k).wait_send() for k in (1, 2, 3)])
 
     @pl.when(owner)
     def _():
@@ -450,29 +500,26 @@
 def finish(act_in, ig_in, gd, gu, act, ig, gdq, guq, gdv, guv):
     act[...] = act_in[...]
     ig[...] = ig_in[...].astype(F32)
-
-    @pl.when(pl.program_id(0) == 0)
-    def _():
-        cols = jnp.concatenate([gd[q, :, 0:192] for q in range(4)], axis=1).T
-        gdq[...] = cols[:, 0:8]
-        gdv[...] = cols[:, 8:16]
-        guq[...] = gu[0:8, 0:192]
-        guv[...] = gu[8:16, 0:192]
+    down = jnp.concatenate([gd[q, :, 0:192] for q in range(4)], axis=1)
+    gdq[...] = down[0:8]
+    gdv[...] = down[8:16]
+    guq[...] = gu[0:8, 0:192]
+    guv[...] = gu[8:16, 0:192]
 
 
 def scratch():
     V, dma = pltpu.VMEM, pltpu.SemaphoreType.DMA
     return [
-        V((S, D), BF), V((S, D), BF), V((D, 192), BF), V((D, 192), BF), V((D, 192), BF),
-        V((D, D), BF), V((D, FF), BF), V((FF, D), BF), V((G, D, GW), BF), V((G, 128, 384), BF),
-        V((S, D), BF), V((S, D), BF),
-        V((S, 1), F32), V((G, S, 256), BF), V((G, S, 256), BF), V((G, GW, S), BF),
+        V((S, D), BF), V((S, D), BF), V((D, D), BF), V((D, FF), BF), V((FF, D), BF), V((G * 576, D), BF),
+        V((G, 16, 384), BF), V((16, D), BF), V((S, D), BF), V((S, D), BF),
+        V((64, S), BF), V((64, S), BF), V((G, S, 256), BF), V((G, S, 256), BF), V((G, GW, S), BF),
         V((3, 2, S, 256), F32), V((12, S, S), BF), V((12, 1, S), F32), V((G, 192, S), BF),
         V((S, D), F32), V((S, 2), F32), V((S, D), BF),
-        V((S, FF), F32), V((S, D), F32), V((G, 192, S), F32), V((3, S, S), BF), V((G, GW, S), BF), V((S, D), BF),
+        V((S, C), F32), V((S, C), F32), V((S, C), BF), V((S, C), BF), V((S, FF), F32), V((S, D), F32),
+        V((G, 192, S), F32), V((3, S, S), BF), V((G * 576, S), BF), V((S, D), BF),
         V((4, 32, 256), F32), V((4, 32, 256), F32), V((32, 256), F32), V((4, 32, 256), F32), V((4, 32, 256), F32),
-        V((4, 16, 256), F32),
-        dma((9,)), dma((2, 4)), dma((2, 4)), dma((2, 4)), dma((2, 4)), dma((2, 4)), dma((2, 4, 4)), dma((2, 4)),
+        V((4, 16, 256), F32), V((16, S), BF),
+        dma((9,)), dma((2, 4)), dma((2, 4)), dma((2, 4)), dma((2, 4)), dma((2, 4, 4)), dma((2, 4, 4)), dma((2, 4)),
         dma((2, 4)), dma((2, 4)), dma((2, 4)), dma((2,)), dma((2, 4)), dma((2, 4)), dma((2, 4)),
     ]
 
@@ -490,25 +537,19 @@
             collective_id=0, has_side_effects=True, vmem_limit_bytes=62 * 2**20
         ),
     )(
-        inputs, cotangent, key_mask, lengths, wq, wk, wv, w_out, w_inner, w_outer,
-        g1[None], b1[None], g2[None], b2[None], dq, uq, dv, uv,
+        inputs, cotangent, key_mask, lengths, wq.T, wk.T, wv.T, w_out, w_inner, w_outer,
+        g1, b1, g2, b2, dq.T, uq, dv.T, uv,
     )
-    one = pl.BlockSpec((1, Q, D), lambda j: (j, 0, 0))
-
-    def whole(*dims):
-        return pl.BlockSpec(dims, lambda j: (0,) * len(dims))
-
     act, ig, gdq, guq, gdv, guv = pl.pallas_call(
         finish,
-        grid=(B,),
         out_shape=(
             shape((B, Q, D), BF), shape((B, Q, D), F32),
-            shape((D, 8), F32), shape((8, 192), F32), shape((D, 8), F32), shape((8, 192), F32),
+            shape((8, D), F32), shape((8, 192), F32), shape((8, D), F32), shape((8, 192), F32),
         ),
-        in_specs=[one, one, whole(4, 16, 256), whole(16, 256)],
-        out_specs=(one, one, whole(D, 8), whole(8, 192), whole(D, 8), whole(8, 192)),
+        in_specs=[vm] * 4,
+        out_specs=(vm,) * 6,
     )(act, ig, gd, gu)
-    return act, ig, gdq, guq, gdv, guv
+    return act, ig, gdq.T, guq, gdv.T, guv
 
 
 def solution(mesh):

time: 118 us -> 95.6 us (0.81)
  local copies, waits for them, and re-layouts: 17.2 us -> 0 us
  Pallas kernels: 99.6 us -> 94.8 us
    unnamed x5 -> x0, local copies, waits for them, and re-layouts: 8.68 us -> none
    broadcast_in_dim x4 -> x0, local copies, waits for them, and re-layouts: 5.07 us -> none  [the longest x1 1.27 us: per_device(): g1[None]]
    pallas_call x2 -> x0, local copies, waits for them, and re-layouts: 3.48 us -> none  [per_device(): pl.pallas_call(finish, grid=(B,), out_shape=(shape((B, Q, D), BF), shape(...]
    pallas_call x1, Pallas kernels: 95.6 us -> 92.3 us  [per_device(): pl.pallas_call(layer, out_shape=(shape((B, Q, D), BF), shape((B, Q, D), B...]
    pallas_call x1, Pallas kernels: 3.99 us -> 2.56 us  [per_device(): pl.pallas_call(finish, out_shape=(shape((B, Q, D), BF), shape((B, Q, D),...]
where the time goes in v2:
time: 95.6 us; the launch traced here: 95.5 us
  Pallas kernels  94.8 us (99%)
    pallas_call x1, Pallas kernels, per_device(): pl.pallas_call(layer, out_shape=(shape((B, Q, D), BF), shape((B, Q, D), B...  92.3 us
    pallas_call x1, Pallas kernels, per_device(): pl.pallas_call(finish, out_shape=(shape((B, Q, D), BF), shape((B, Q, D),...  2.56 us

profile of v2, /device:TPU:0, one launch (start us, length us, event | category | flops | bytes accessed | tf_op | source)
XLA Modules:
  0.0 95.5 jit_solution(6072336774142788001)
XLA Ops:
  0.6 92.3 %shard_map.217 = (bf16[3,128,768]{2,1,0:T(8,128)(2,1)}, bf16[3,128,768]{2,1,0:T(8,128)(2,1)}, f32[4,16,256]{2,1,0:T(8,128)}, f32[16,256]{1,0:T(8,128)}) custom-call(bf16[3,128,768]{2,1,0:T(8,128)(2,1)} %inputs.1, bf16[3,128,768]{2,1,0:T(8,128)(2,1)} %cot.1, s32[3,512]{1,0:T(4,128)} %kmask.1, s32[3]{0:T(128)} %lengths.1, bf16[192,768]{1,0:T(8,128)(2,1)} %bitcast.7, ...), custom_call_target="tpu_custom_call" | custom-call | tf_op jit(solution)/shard_map/pallas_call | solution.py:530
  92.9 2.6 %shard_map.218 = (bf16[3,128,768]{2,1,0:T(8,128)(2,1)}, f32[3,128,768]{2,1,0:T(8,128)}, f32[8,768]{1,0:T(8,128)}, f32[8,192]{1,0:T(8,128)}, f32[8,768]{1,0:T(8,128)}, /*index=5*/f32[8,192]{1,0:T(8,128)}) custom-call(bf16[3,128,768]{2,1,0:T(8,128)(2,1)} %get-tuple-element.16.act_in, bf16[3,128,768]{2,1,0:T(8,128)(2,1)} %get-tuple-element.17.ig_in, ...), custom_call_target="tpu_custom_call" | custom-call | tf_op jit(solution)/shard_map/pallas_call | solution.py:543

commit v3 on v2

v3 whole, which is shorter than its diff:
```python
import functools

import jax
import jax.numpy as jnp
from jax import lax
from jax.experimental import pallas as pl
from jax.experimental.pallas import tpu as pltpu
from jax.sharding import Mesh
from jax.sharding import PartitionSpec as P

BF, F32 = jnp.bfloat16, jnp.float32
S, D, FF, HD, G = 512, 768, 3072, 64, 4
B, Q = 3, 128
GW = 640
C = 512
NT = (((1,), (1,)), ((), ()))
DP = ("dp_0", "dp_1", "dp_2")
MESH = pl.DeviceIdType.MESH


def nn(a, b):
    return jnp.dot(a, b, preferred_element_type=F32)


def nt(a, b):
    return lax.dot_general(a, b, NT, preferred_element_type=F32)


def middle(x, wg, mid):
    mid[0:16, :] = nt(wg[576:592, :], x[...]).astype(BF)
    mid[16:64, :] = jnp.zeros((48, S), BF)


def project(g, x, wg, up, mid, bias, knat, vnat, yt):
    y = nt(wg[GW * g : GW * g + 576, :], x[...])
    upt = jnp.concatenate([up[g], jnp.zeros((112, 384), BF)], axis=0).T
    qv = y[0:384] + nn(upt[:, 0:64], mid[...])
    vt = qv[192:384].astype(BF)
    yt[g, 0:192, :] = (qv[0:192].astype(BF).astype(F32) * 0.125).astype(BF)
    yt[g, 192:384, :] = vt
    vnat[g] = jnp.concatenate([jnp.zeros((64, S), BF), vt], axis=0).T
    kt = jnp.concatenate([y[384:576].astype(BF), bias[...]], axis=0)
    yt[g, 384:GW, :] = kt
    knat[g] = kt.T


def pad_rows(piece, before, total):
    parts, lanes = [], piece.shape[1]
    if before:
        parts.append(jnp.zeros((before, lanes), BF))
    parts.append(piece)
    after = total - before - piece.shape[0]
    if after:
        parts.append(jnp.zeros((after, lanes), BF))
    return jnp.concatenate(parts, axis=0)


def staged(units, *stages):
    for step in range(len(units) + len(stages) - 1):
        for n, stage in enumerate(stages):
            if 0 <= step - n < len(units):
                stage(step - n, *units[step - n])


def half_cols(half):
    return slice(256 * half, 256 * half + 256)


def attend(units, place, knat, yt, sscr, p, rl, ctxt):
    maxima = {}

    def scores(u, g, j, half):
        cols = half_cols(half)
        last = (lax.broadcasted_iota(jnp.int32, (64, 256), 0) == 63).astype(BF)
        rhs = jnp.concatenate([pad_rows(yt[g, 64 * j : 64 * j + 64, cols], 64 * j, 192), last], axis=0)
        s = nn(knat[g], rhs)
        sscr[u % 3] = s
        maxima[u] = jnp.max(s, axis=0, keepdims=True)

    def weights(u, g, j, half):
        p[g * 3 + j, :, half_cols(half)] = jnp.exp(sscr[u % 3] - maxima[u]).astype(BF)

    def mix(u, g, j, half):
        cols = half_cols(half)
        vt = jnp.concatenate([yt[g, 192 + 64 * j : 256 + 64 * j, :], jnp.ones((16, S), BF)], axis=0)
        ot = nn(vt, p[g * 3 + j, :, cols])
        rinv = 1.0 / ot[64:65]
        rl[g * 3 + j, :, cols] = rinv
        ctxt[place(g), 64 * j : 64 * j + 64, cols] = (ot[0:64] * rinv).astype(BF)

    staged(units, scores, weights, mix)


def attend_back(units, place, vnat, yt, p, rl, ctxt, dot_ref, dosc, dsscr, dkv, dyt):
    def grads(u, g, j, half):
        rows, cols = slice(64 * j, 64 * j + 64), half_cols(half)
        do = (dot_ref[place(g), rows, cols].astype(F32) * rl[g * 3 + j, :, cols]).astype(BF)
        dosc[u % 3] = do
        dsum = jnp.sum(do.astype(F32) * ctxt[place(g), rows, cols].astype(F32), axis=0, keepdims=True)
        dp = nn(vnat[g], pad_rows(do, 64 + 64 * j, 256))
        dsscr[u % 3] = (p[g * 3 + j, :, cols].astype(F32) * (dp - dsum)).astype(BF)

    def products(u, g, j, half):
        h, cols, at = g * 3 + j, half_cols(half), GW * g + 64 * j
        ds = dsscr[u % 3]
        dv = nt(dosc[u % 3], p[h, :, cols])
        dk = nt(yt[g, 64 * j : 64 * j + 64, cols], ds)
        dyt[at : at + 64, cols] = (nn(yt[g, 384 + 64 * j : 448 + 64 * j, :], ds) * 0.125).astype(BF)
        if half == 0:
            dkv[h, 0], dkv[h, 1] = dv, dk
        else:
            dyt[at + 192 : at + 256, :] = (dkv[h, 0] + dv).astype(BF)
            dyt[at + 384 : at + 448, :] = (dkv[h, 1] + dk).astype(BF)

    staged(units, grads, products)


def gelu_pair(v):
    e = jnp.exp(v * v * -0.5)
    t = 1.0 / (1.0 + 0.23164189 * jnp.abs(v))
    tail = t * (0.127414796 + t * (-0.142248368 + t * (0.7107068705 + t * (-0.7265760135 + t * 0.5307027145)))) * e
    cdf = jnp.where(v >= 0.0, 1.0 - tail, tail)
    return v * cdf, cdf + v * (e * 0.3989422804)


def norm(h):
    mean = jnp.mean(h, axis=-1, keepdims=True)
    c = h - mean
    r = lax.rsqrt(jnp.mean(c * c, axis=-1, keepdims=True) + 1e-5)
    return c * r, r


def norm_back(n, xhat, r):
    return r * (n - jnp.mean(n, axis=-1, keepdims=True) - xhat * jnp.mean(n * xhat, axis=-1, keepdims=True))


def chunk(c):
    return pl.ds(pl.multiple_of(c * C, C), C)


def feed_forward(n1b, wi, wt, hs, a, dact, acc):
    n = FF // C
    for c in range(n + 1):
        if c < n:
            hs[c % 2] = nn(n1b[...], wi[:, C * c : C * c + C])
        if c > 0:
            cols = slice(C * (c - 1), C * c)
            v, d = gelu_pair(hs[(c - 1) % 2])
            a[:, cols] = v.astype(BF)
            dact[:, cols] = d
            acc[...] += nn(a[:, cols], wt[cols, :])


def feed_back(gnb, wi, wt, a, dact, acc):
    for c in range(FF // C):
        cols = slice(C * c, C * c + C)
        a[:, cols] = (nt(gnb[...], wt[cols, :]) * dact[:, cols]).astype(BF)
    acc[...] += nt(a[...], wi[...])
def remote(src, dst, send, recv, **where):
    return pltpu.make_async_remote_copy(
        src_ref=src, dst_ref=dst, send_sem=send, recv_sem=recv, device_id=where, device_id_type=MESH
    )


def layer(
    inputs, cot, kmask, lengths, wq, wk, wv, w_out, w_inner, w_outer, g1, b1, g2, b2, dq, uq, dv, uv,
    act_out, ig_out, gd_out, gu_out,
    x, ct, wo, wi, wt, wg, up, act, igb,
    bias, mid, knat, vnat, yt, sscr, p, rl, ctxt, xhat1, xhat2, r1s, n1b, hs, a, dact, acc,
    dot_ref, dosc, dsscr, dkv, dyt, gnb,
    msg, redz, redc, redx, redy, gdp,
    lsem, xsem, csem, wsem, usem, w1, w2, w3, asem, isem, gz, gc, gx, gy, gf,
):
    ix, iy, ic, iz = (lax.axis_index(n) for n in ("dp_0", "dp_1", "dp_2", "heads"))
    rank = lax.rem(iz + 2 * ic, 4)
    owner = rank < 3
    mine = jnp.minimum(rank, 2)

    def z_of(r):
        return lax.rem(r + 2 * ic, 4)

    def turn(i, by):
        return lax.rem(i + by, 4)

    def place(g):
        return turn(iz, g)

    barrier = pltpu.get_barrier_semaphore()
    peers = [{"dp_2": 1 - ic}]
    for i in (1, 2, 3):
        peers += [{"heads": turn(iz, i)}, {"dp_0": turn(ix, i)}, {"dp_1": turn(iy, i)}]
    for where in peers:
        pl.semaphore_signal(barrier, inc=1, device_id=where, device_id_type=MESH)
    weights = (wq, wv, wk)
    loads = [pltpu.make_async_copy(w, wg.at[pl.ds(192 * n, 192)], lsem.at[n]) for n, w in enumerate(weights)]
    late = [
        pltpu.make_async_copy(w, v, lsem.at[3 + n]) for n, (w, v) in enumerate(((w_out, wo), (w_inner, wi), (w_outer, wt)))
    ]
    pl.semaphore_wait(barrier, 10)

    la, lb = ix * (1 - ic) + iy * ic, iy * (1 - ic) + ix * ic
    slice_at = 3 * lb + la
    holds = la < 3

    def part(k, at, count, core=ic):
        rows = pl.ds(pl.multiple_of(GW * k + at, 16), count)
        return wg.at[rows, pl.ds(pl.multiple_of(384 * core, 128), 384)]

    def along_a(i):
        return {"dp_0": turn(ix, i * (1 - ic)), "dp_1": turn(iy, i * ic)}

    def along_b(i):
        return {"dp_0": turn(ix, i * ic), "dp_1": turn(iy, i * (1 - ic))}

    def over_z(i, src=None):
        src = part(0, 48 * slice_at, 48) if src is None else src
        return remote(src, part(4 - i, 48 * slice_at, 48), wsem.at[0, i], wsem.at[1, 4 - i], heads=turn(iz, i))

    def first(k, i):
        block = part(k, 48 * slice_at, 48)
        return remote(block, block, w1.at[0, k, i], w1.at[1, k, i], **along_a(i))

    def second(k, i):
        block = part(k, 144 * lb, 144)
        return remote(block, block, w2.at[0, k, i], w2.at[1, k, i], **along_b(i))

    def third(k, core=ic):
        block = part(k, 0, 576, core)
        return remote(block, block, w3.at[0, k], w3.at[1, k], dp_2=1 - ic)

    def when_holds(do):
        pl.when(holds)(do)

    def join(k):
        for i in (1, 2, 3):
            second(k, i).wait_recv()
        third(k).start()

    for m in range(3):
        @pl.when(jnp.logical_and(holds, slice_at // 4 == m))
        def _():
            rows = pl.ds(pl.multiple_of(48 * lax.rem(slice_at, 4), 16), 48)
            for i in (1, 2, 3):
                over_z(i, weights[m].at[rows, pl.ds(pl.multiple_of(384 * ic, 128), 384)]).start()

    def slot(ref, r):
        return ref.at[pl.ds(pl.multiple_of(r * Q, Q), Q)]

    def spread(src, dst, sem):
        for j in range(B):
            @pl.when(rank != j)
            def _():
                remote(src.at[j], slot(dst, rank), sem.at[0, j], sem.at[1, rank], heads=z_of(j)).start()

            @pl.when(rank == j)
            def _():
                pltpu.make_async_copy(src.at[j], slot(dst, rank), sem.at[1, j]).start()

    def spread_wait(src, dst, sem):
        @pl.when(owner)
        def _():
            for r in range(4):
                pltpu.make_async_copy(src.at[0], dst.at[pl.ds(r * Q, Q)], sem.at[1, r]).wait()

    def spread_end(src, dst, sem):
        for j in range(B):
            @pl.when(rank != j)
            def _():
                remote(src.at[j], slot(dst, rank), sem.at[0, j], sem.at[1, rank], heads=z_of(j)).wait_send()

    spread(inputs, x, xsem)
    for c in loads:
        c.start()

    zero8 = jnp.zeros((8, 192), F32)
    both = jnp.concatenate(
        [
            jnp.concatenate([uq[...].astype(F32), zero8], axis=1),
            jnp.concatenate([zero8, uv[...].astype(F32)], axis=1),
        ],
        axis=0,
    )
    up[0] = (2.0 * both).astype(BF)
    ups = [
        remote(up.at[0], up.at[4 - i], usem.at[0, i], usem.at[1, 4 - i], heads=turn(iz, i)) for i in (1, 2, 3)
    ]
    for c in ups:
        c.start()
    down = jnp.concatenate([dq[...].astype(F32), dv[...].astype(F32)], axis=0).astype(BF)
    for g in range(G):
        wg[GW * g + 576 : GW * g + GW, :] = jnp.concatenate(
            [down if g == 0 else jnp.zeros((16, D), BF), jnp.zeros((48, D), BF)], axis=0
        )

    @when_holds
    def _():
        for k in (1, 2, 3):
            pltpu.make_async_copy(part(k, 0, 48), part(k, 0, 48), wsem.at[1, k]).wait()
            for i in (1, 2, 3):
                first(k, i).start()

    for k in (1, 2, 3):
        for i in (1, 2, 3):
            @pl.when(turn(la, 4 - i) < 3)
            def _():
                first(k, i).wait_recv()
        for i in (1, 2, 3):
            second(k, i).start()
    spread(cot, ct, csem)
    for c in late:
        c.start()

    row = jnp.where(mine == 0, kmask[0:1], jnp.where(mine == 1, kmask[1:2], kmask[2:3]))
    row = jnp.where(ic == 0, row, jnp.concatenate([row[:, 256:512], row[:, 0:256]], axis=1))
    row = jnp.where(row > 0, 0.0, -1e30).astype(F32)
    bias[...] = jnp.where(lax.broadcasted_iota(jnp.int32, (64, S), 0) == 63, row, 0.0).astype(BF)
    for c in loads:
        c.wait()
    for c in ups:
        c.wait_recv()
    join(1)
    spread_wait(inputs, x, xsem)

    def project_group(g):
        project(g, x, wg, up, mid, bias, knat, vnat, yt)

    def attend_some(units):
        attend(units, place, knat, yt, sscr, p, rl, ctxt)

    @pl.when(owner)
    def _():
        middle(x, wg, mid)
        project_group(0)

    for g in range(3):
        if g < 2:
            join(g + 2)
        third(g + 1, 1 - ic).wait_recv()

        @pl.when(owner)
        def _():
            project_group(g + 1)
            attend_some([(g, j, 1) for j in range(3)])

    for c in late:
        c.wait()

    def rows_of(src, t):
        return src.at[pl.ds(pl.multiple_of(t * Q, Q), Q)]

    def sent_back(src, dst, sem, i):
        return remote(rows_of(src, turn(rank, i)), dst.at[mine], sem.at[0, i], sem.at[1, mine], heads=turn(iz, i))

    def back(src, dst, sem):
        for i in (1, 2, 3):
            sent_back(src, dst, sem, i).start()
        pltpu.make_async_copy(rows_of(src, mine), dst.at[mine], sem.at[1, mine]).start()

    def back_end(src, dst, sem):
        for j in range(B):
            pltpu.make_async_copy(src.at[pl.ds(0, Q)], dst.at[j], sem.at[1, j]).wait()

        @pl.when(owner)
        def _():
            for i in (1, 2, 3):
                sent_back(src, dst, sem, i).wait_send()

    @pl.when(owner)
    def _():
        attend_some([(3, j, 1) for j in range(3)] + [(g, j, 0) for g in range(G) for j in range(3)])
        ctx = jnp.concatenate([ctxt[g].T for g in range(G)], axis=1)
        xh, r = norm(x[...].astype(F32) + nn(ctx, wo[...]))
        xhat1[...] = xh
        r1s[...] = r
        n1v = xh * g1[...][None] + b1[...][None]
        n1b[...] = n1v.astype(BF)
        acc[...] = n1v
        feed_forward(n1b, wi, wt, hs, a, dact, acc)
        xh2, r2 = norm(acc[...])
        act[...] = (xh2 * g2[...][None] + b2[...][None]).astype(BF)
        xhat2[...] = xh2
        back(act, act_out, asem)
        acc[:, 0:1] = r2

    spread_wait(cot, ct, csem)

    @pl.when(owner)
    def _():
        limit = lengths[mine]
        at = lax.broadcasted_iota(jnp.int32, (Q, 1), 0)
        valid = jnp.concatenate([at + z_of(t) * Q < limit for t in range(4)], axis=0)
        tangent = jnp.where(valid, ct[...].astype(F32), 0.0)
        gs = norm_back(tangent * g2[...][None], xhat2[...], acc[:, 0:1])
        gnb[...] = gs.astype(BF)
        acc[...] = gs
        feed_back(gnb, wi, wt, a, dact, acc)
        gf1 = norm_back(acc[...] * g1[...][None], xhat1[...], r1s[...])
        acc[...] = gf1
        gfb = gf1.astype(BF)
        for g in range(G):
            dot_ref[g] = nt(wo[192 * g : 192 * g + 192, :], gfb)
        for half in range(2):
            attend_back([(g, j, half) for g in range(G) for j in range(3)], place, vnat, yt, p, rl, ctxt, dot_ref, dosc,
                        dsscr, dkv, dyt)
        gm = jnp.zeros((16, S), F32)
        first_rows = lax.broadcasted_iota(jnp.int32, (16, 192), 0) < 8
        for g in range(G):
            dqv = dyt[GW * g : GW * g + 384, :]
            gu = nt(mid[0:16, :], dqv)
            msg[g, 0:16, 0:192] = jnp.where(first_rows, gu[:, 0:192], gu[:, 192:384]) * 2.0
            gm = gm + nn(up[g], dqv)
        gmb = gm.astype(BF)
        gd = nn(gmb, x[...])
        for q in range(4):
            gdp[q, :, 0:192] = gd[:, 192 * q : 192 * q + 192]
        for k in range(G):
            msg[k, 16:32, 0:192] = gdp[place(k), :, 0:192]
            dyt[GW * k + 576 : GW * k + GW, :] = jnp.concatenate(
                [gmb if k == 0 else jnp.zeros((16, S), BF), jnp.zeros((48, S), BF)], axis=0
            )

    zsum = [remote(msg.at[i], redz.at[4 - i], gz.at[0, i], gz.at[1, 4 - i], heads=turn(iz, i)) for i in (1, 2, 3)]
    core_sum = remote(redz.at[0], redc, gc.at[0], gc.at[1], dp_2=1 - ic)

    def line(buf, sem, axis, me):
        return [remote(buf.at[me], buf.at[me], sem.at[0, i], sem.at[1, i], **{axis: turn(me, i)}) for i in (1, 2, 3)]

    over_x, over_y = line(redx, gx, "dp_0", ix), line(redy, gy, "dp_1", iy)
    over_q = [remote(gd_out.at[iz], gd_out.at[iz], gf.at[0, i], gf.at[1, i], heads=turn(iz, i)) for i in (1, 2, 3)]

    def start(copies):
        for c in copies:
            c.start()

    def finish_copies(copies):
        for c in copies:
            c.wait()

    @pl.when(owner)
    def _():
        start(zsum)
        redz[0] = msg[0]
        for g in range(G):
            a[:, GW * g : GW * g + GW] = dyt[GW * g : GW * g + GW, :].T
        for half in (1, 0):
            rows = half_cols(half)
            igb[rows, :] = (acc[rows, :] + nn(a[rows, 0 : G * GW], wg[...])).astype(BF)
        back(igb, ig_out, isem)

    @pl.when(rank == 3)
    def _():
        redz[0] = jnp.zeros((32, 256), F32)

    for i in (1, 2, 3):
        @pl.when(turn(rank, i) != 3)
        def _():
            pltpu.make_async_copy(msg.at[i], redz.at[i], gz.at[1, i]).wait()
            redz[0] += redz[i]

    core_sum.start()
    core_sum.wait()
    redx[ix] = redz[0] + redc[...]
    start(over_x)
    finish_copies(over_x)
    redy[iy] = redx[0] + redx[1] + redx[2] + redx[3]
    start(over_y)
    finish_copies(over_y)
    total = redy[0] + redy[1] + redy[2] + redy[3]
    gu_out[...] = total[0:16]
    gd_out[iz] = total[16:32]
    start(over_q)
    finish_copies(over_q)

    back_end(act, act_out, asem)
    back_end(igb, ig_out, isem)
    spread_end(inputs, x, xsem)
    spread_end(cot, ct, csem)
    for c in ups:
        c.wait_send()

    @when_holds
    def _():
        for i in (1, 2, 3):
            over_z(i).wait_send()
            for k in (1, 2, 3):
                first(k, i).wait_send()

    for k in (1, 2, 3):
        for i in (1, 2, 3):
            second(k, i).wait_send()
        third(k).wait_send()

    @pl.when(owner)
    def _():
        for c in zsum:
            c.wait_send()


def finish(act_in, ig_in, gd, gu, act, ig, gdq, guq, gdv, guv):
    act[...] = act_in[...]
    ig[...] = ig_in[...].astype(F32)
    down = jnp.concatenate([gd[q, :, 0:192] for q in range(4)], axis=1)
    gdq[...] = down[0:8]
    gdv[...] = down[8:16]
    guq[...] = gu[0:8, 0:192]
    guv[...] = gu[8:16, 0:192]


def scratch():
    V, dma = pltpu.VMEM, pltpu.SemaphoreType.DMA
    return [
        V((S, D), BF), V((S, D), BF), V((D, D), BF), V((D, FF), BF), V((FF, D), BF), V((G * GW, D), BF),
        V((G, 16, 384), BF), V((S, D), BF), V((S, D), BF),
        V((64, S), BF), V((64, S), BF), V((G, S, 256), BF), V((G, S, 256), BF), V((G, GW, S), BF),
        V((3, S, 256), F32), V((12, S, S), BF), V((12, 1, S), F32), V((G, 192, S), BF),
        V((S, D), F32), V((S, D), F32), V((S, 1), F32), V((S, D), BF),
        V((2, S, C), F32), V((S, FF), BF), V((S, FF), F32), V((S, D), F32),
        V((G, 192, S), F32), V((3, 64, 256), BF), V((3, S, 256), BF), V((12, 2, 64, S), F32), V((G * GW, S), BF),
        V((S, D), BF),
        V((4, 32, 256), F32), V((4, 32, 256), F32), V((32, 256), F32), V((4, 32, 256), F32), V((4, 32, 256), F32),
        V((4, 16, 256), F32),
        dma((6,)), dma((2, 4)), dma((2, 4)), dma((2, 4)), dma((2, 4)), dma((2, 4, 4)), dma((2, 4, 4)), dma((2, 4)),
        dma((2, 4)), dma((2, 4)), dma((2, 4)), dma((2,)), dma((2, 4)), dma((2, 4)), dma((2, 4)),
    ]


def per_device(inputs, key_mask, lengths, cotangent, wq, wk, wv, w_out, w_inner, w_outer, g1, b1, g2, b2, dq, uq, dv, uv):
    vm, hbm = pl.BlockSpec(memory_space=pltpu.VMEM), pl.BlockSpec(memory_space=pl.ANY)
    shape = jax.ShapeDtypeStruct
    act, ig, gd, gu = pl.pallas_call(
        layer,
        out_shape=(shape((B, Q, D), BF), shape((B, Q, D), BF), shape((4, 16, 256), F32), shape((16, 256), F32)),
        in_specs=[hbm, hbm, vm, pl.BlockSpec(memory_space=pltpu.SMEM)] + [hbm] * 6 + [vm] * 8,
        out_specs=(hbm, hbm, vm, vm),
        scratch_shapes=scratch(),
        compiler_params=pltpu.CompilerParams(
            collective_id=0, has_side_effects=True, vmem_limit_bytes=62 * 2**20
        ),
    )(
        inputs, cotangent, key_mask, lengths, wq.T, wk.T, wv.T, w_out, w_inner, w_outer,
        g1, b1, g2, b2, dq.T, uq, dv.T, uv,
    )
    act, ig, gdq, guq, gdv, guv = pl.pallas_call(
        finish,
        out_shape=(
            shape((B, Q, D), BF), shape((B, Q, D), F32),
            shape((8, D), F32), shape((8, 192), F32), shape((8, D), F32), shape((8, 192), F32),
        ),
        in_specs=[vm] * 4,
        out_specs=(vm,) * 6,
    )(act, ig, gd, gu)
    return act, ig, gdq.T, guq, gdv.T, guv


def solution(mesh):
    finer = Mesh(
        mesh.devices.reshape(4, 4, 2, mesh.shape["heads"]), ("dp_0", "dp_1", "dp_2", "heads")
    )
    rows, cols, same = P(DP, "heads", None), P(None, "heads"), P()
    return jax.shard_map(
        per_device,
        mesh=finer,
        in_specs=(rows, P(DP, None), P(DP), rows, cols, cols, cols) + (same,) * 8 + (cols, same, cols),
        out_specs=(rows, rows, same, cols, same, cols),
        check_vma=False,
    )
```

time: 95.6 us -> 83.3 us (0.87)
  Pallas kernels: 94.8 us -> 82.2 us
    pallas_call x1, Pallas kernels: 92.3 us -> 79.7 us  [per_device(): pl.pallas_call(layer, out_shape=(shape((B, Q, D), BF), shape((B, Q, D), B...]
where the time goes in v3:
time: 83.3 us; the launch traced here: 82.9 us
  Pallas kernels  82.2 us (99%)
    pallas_call x1, Pallas kernels, per_device(): pl.pallas_call(layer, out_shape=(shape((B, Q, D), BF), shape((B, Q, D), B...  79.7 us
    pallas_call x1, Pallas kernels, per_device(): pl.pallas_call(finish, out_shape=(shape((B, Q, D), BF), shape((B, Q, D),...  2.56 us

profile of v3, /device:TPU:0, one launch (start us, length us, event | category | flops | bytes accessed | tf_op | source)
XLA Modules:
  0.0 82.9 jit_solution(6116275109521322799)
XLA Ops:
  0.6 79.7 %shard_map.217 = (bf16[3,128,768]{2,1,0:T(8,128)(2,1)}, bf16[3,128,768]{2,1,0:T(8,128)(2,1)}, f32[4,16,256]{2,1,0:T(8,128)}, f32[16,256]{1,0:T(8,128)}) custom-call(bf16[3,128,768]{2,1,0:T(8,128)(2,1)} %inputs.1, bf16[3,128,768]{2,1,0:T(8,128)(2,1)} %cot.1, s32[3,512]{1,0:T(4,128)} %kmask.1, s32[3]{0:T(128)} %lengths.1, bf16[192,768]{1,0:T(8,128)(2,1)} %bitcast.7, ...), custom_call_target="tpu_custom_call" | custom-call | tf_op jit(solution)/shard_map/pallas_call | solution.py:530
  80.3 2.6 %shard_map.218 = (bf16[3,128,768]{2,1,0:T(8,128)(2,1)}, f32[3,128,768]{2,1,0:T(8,128)}, f32[8,768]{1,0:T(8,128)}, f32[8,192]{1,0:T(8,128)}, f32[8,768]{1,0:T(8,128)}, /*index=5*/f32[8,192]{1,0:T(8,128)}) custom-call(bf16[3,128,768]{2,1,0:T(8,128)(2,1)} %get-tuple-element.16.act_in, bf16[3,128,768]{2,1,0:T(8,128)(2,1)} %get-tuple-element.17.ig_in, ...), custom_call_target="tpu_custom_call" | custom-call | tf_op jit(solution)/shard_map/pallas_call | solution.py:543

commit v4 on v3

--- a/solution.py
+++ b/solution.py
@@ -163,13 +163,13 @@
 
 
 def layer(
-    inputs, cot, kmask, lengths, wq, wk, wv, w_out, w_inner, w_outer, g1, b1, g2, b2, dq, uq, dv, uv,
+    inputs, cot, kmask_in, lengths, wq, wk, wv, w_out, w_inner, w_outer, g1_in, b1_in, g2_in, b2_in, dq_in, uq_in, dv_in, uv_in,
     act_out, ig_out, gd_out, gu_out,
-    x, ct, wo, wi, wt, wg, up, act, igb,
+    kmask, g1, b1, g2, b2, dq, uq, dv, uv, x, ct, wo, wi, wt, wg, up, act, igb,
     bias, mid, knat, vnat, yt, sscr, p, rl, ctxt, xhat1, xhat2, r1s, n1b, hs, a, dact, acc,
     dot_ref, dosc, dsscr, dkv, dyt, gnb,
-    msg, redz, redc, redx, redy, gdp,
-    lsem, xsem, csem, wsem, usem, w1, w2, w3, asem, isem, gz, gc, gx, gy, gf,
+    msg, redz, redx, redy, gdp,
+    lsem, xsem, csem, wsem, usem, w1, w2, w3, asem, isem, gz, gx, gy, gf,
 ):
     ix, iy, ic, iz = (lax.axis_index(n) for n in ("dp_0", "dp_1", "dp_2", "heads"))
     rank = lax.rem(iz + 2 * ic, 4)
@@ -182,6 +182,9 @@
     def turn(i, by):
         return lax.rem(i + by, 4)
 
+    def turn2(i, by):
+        return lax.rem(i + by, 2)
+
     def place(g):
         return turn(iz, g)
 
@@ -189,6 +192,7 @@
     peers = [{"dp_2": 1 - ic}]
     for i in (1, 2, 3):
         peers += [{"heads": turn(iz, i)}, {"dp_0": turn(ix, i)}, {"dp_1": turn(iy, i)}]
+    peers += [{"heads": turn(iz, i), "dp_2": 1 - ic} for i in (1, 2, 3)]
     for where in peers:
         pl.semaphore_signal(barrier, inc=1, device_id=where, device_id_type=MESH)
     weights = (wq, wv, wk)
@@ -196,52 +200,112 @@
     late = [
         pltpu.make_async_copy(w, v, lsem.at[3 + n]) for n, (w, v) in enumerate(((w_out, wo), (w_inner, wi), (w_outer, wt)))
     ]
-    pl.semaphore_wait(barrier, 10)
+    small = [
+        pltpu.make_async_copy(src, dst, lsem.at[6 + n])
+        for n, (src, dst) in enumerate(
+            ((kmask_in, kmask), (g1_in, g1), (b1_in, b1), (g2_in, g2), (b2_in, b2),
+             (dq_in, dq), (uq_in, uq), (dv_in, dv), (uv_in, uv))
+        )
+    ]
+    for c in loads + small:
+        c.start()
+    pl.semaphore_wait(barrier, 13)
+    for c in loads + small:
+        c.wait()
 
     la, lb = ix * (1 - ic) + iy * ic, iy * (1 - ic) + ix * ic
-    slice_at = 3 * lb + la
-    holds = la < 3
 
     def part(k, at, count, core=ic):
         rows = pl.ds(pl.multiple_of(GW * k + at, 16), count)
         return wg.at[rows, pl.ds(pl.multiple_of(384 * core, 128), 384)]
 
+    def block(k, b, half=None, core=ic):
+        at, count = ((0, 144), (0, 80), (80, 64))[0 if half is None else half + 1]
+        return part(k, 144 * b + at, count, core)
+
     def along_a(i):
         return {"dp_0": turn(ix, i * (1 - ic)), "dp_1": turn(iy, i * ic)}
 
     def along_b(i):
         return {"dp_0": turn(ix, i * ic), "dp_1": turn(iy, i * (1 - ic))}
 
-    def over_z(i, src=None):
-        src = part(0, 48 * slice_at, 48) if src is None else src
-        return remote(src, part(4 - i, 48 * slice_at, 48), wsem.at[0, i], wsem.at[1, 4 - i], heads=turn(iz, i))
-
-    def first(k, i):
-        block = part(k, 48 * slice_at, 48)
-        return remote(block, block, w1.at[0, k, i], w1.at[1, k, i], **along_a(i))
-
-    def second(k, i):
-        block = part(k, 144 * lb, 144)
-        return remote(block, block, w2.at[0, k, i], w2.at[1, k, i], **along_b(i))
-
-    def third(k, core=ic):
-        block = part(k, 0, 576, core)
-        return remote(block, block, w3.at[0, k], w3.at[1, k], dp_2=1 - ic)
-
-    def when_holds(do):
-        pl.when(holds)(do)
+    over_z = remote(block(0, lb), block(la, lb), wsem.at[0], wsem.at[1], heads=turn(iz, 4 - la))
+
+    def ring_a(n, k):
+        what = block(k, lb, n - 2 if n > 1 else None)
+        return remote(what, what, w1.at[0, n], w1.at[1, n], **along_a(3 if n % 2 else 1))
+
+    def ring_b(n, k, b):
+        what = block(k, b, n - 2 if n > 1 else None)
+        return remote(what, what, w2.at[0, n, k], w2.at[1, n, k], **along_b(3 if n % 2 else 1))
+
+    def to_core(k, b, core=ic):
+        what = block(k, b, None, core)
+        return remote(what, what, w3.at[0, k, b], w3.at[1, k, b], dp_2=1 - ic)
+
+    def got_line(k):
+        ring_b(0, k, lb).start()
+        ring_b(1, k, lb).start()
+        to_core(k, lb).start()
+
+    def join_line():
+        @pl.when(la > 0)
+        def _():
+            over_z.wait_recv()
+            ring_a(0, la).start()
+            ring_a(1, la).start()
+            got_line(la)
+
+        for n, k in ((0, turn(la, 3)), (1, turn(la, 1))):
+            @pl.when(k > 0)
+            def _():
+                ring_a(n, k).wait_recv()
+                ring_a(n + 2, k).start()
+                got_line(k)
+
+        far = turn(la, 2)
+
+        @pl.when(far > 0)
+        def _():
+            ring_a(2, far).wait_recv()
+            ring_a(3, far).wait_recv()
+            got_line(far)
 
     def join(k):
-        for i in (1, 2, 3):
-            second(k, i).wait_recv()
-        third(k).start()
-
-    for m in range(3):
-        @pl.when(jnp.logical_and(holds, slice_at // 4 == m))
+        for n, b in ((0, turn(lb, 3)), (1, turn(lb, 1))):
+            ring_b(n, k, b).wait_recv()
+            ring_b(n + 2, k, b).start()
+            to_core(k, b).start()
+        far = turn(lb, 2)
+        ring_b(2, k, far).wait_recv()
+        ring_b(3, k, far).wait_recv()
+        to_core(k, far).start()
+
+    def arrived(k):
+        for b in range(4):
+            to_core(k, b, 1 - ic).wait_recv()
+
+    def weights_end():
+        @pl.when(la > 0)
         def _():
-            rows = pl.ds(pl.multiple_of(48 * lax.rem(slice_at, 4), 16), 48)
-            for i in (1, 2, 3):
-                over_z(i, weights[m].at[rows, pl.ds(pl.multiple_of(384 * ic, 128), 384)]).start()
+            over_z.wait_send()
+            ring_a(0, la).wait_send()
+            ring_a(1, la).wait_send()
+
+        for n, k in ((0, turn(la, 3)), (1, turn(la, 1))):
+            @pl.when(k > 0)
+            def _():
+                ring_a(n + 2, k).wait_send()
+
+        for k in (1, 2, 3):
+            for n in range(4):
+                ring_b(n, k, lb).wait_send()
+            for b in range(4):
+                to_core(k, b).wait_send()
+
+    @pl.when(la > 0)
+    def _():
+        over_z.start()
 
     def slot(ref, r):
         return ref.at[pl.ds(pl.multiple_of(r * Q, Q), Q)]
@@ -269,8 +333,6 @@
                 remote(src.at[j], slot(dst, rank), sem.at[0, j], sem.at[1, rank], heads=z_of(j)).wait_send()
 
     spread(inputs, x, xsem)
-    for c in loads:
-        c.start()
 
     zero8 = jnp.zeros((8, 192), F32)
     both = jnp.concatenate(
@@ -292,20 +354,7 @@
             [down if g == 0 else jnp.zeros((16, D), BF), jnp.zeros((48, D), BF)], axis=0
         )
 
-    @when_holds
-    def _():
-        for k in (1, 2, 3):
-            pltpu.make_async_copy(part(k, 0, 48), part(k, 0, 48), wsem.at[1, k]).wait()
-            for i in (1, 2, 3):
-                first(k, i).start()
-
-    for k in (1, 2, 3):
-        for i in (1, 2, 3):
-            @pl.when(turn(la, 4 - i) < 3)
-            def _():
-                first(k, i).wait_recv()
-        for i in (1, 2, 3):
-            second(k, i).start()
+    join_line()
     spread(cot, ct, csem)
     for c in late:
         c.start()
@@ -314,8 +363,6 @@
     row = jnp.where(ic == 0, row, jnp.concatenate([row[:, 256:512], row[:, 0:256]], axis=1))
     row = jnp.where(row > 0, 0.0, -1e30).astype(F32)
     bias[...] = jnp.where(lax.broadcasted_iota(jnp.int32, (64, S), 0) == 63, row, 0.0).astype(BF)
-    for c in loads:
-        c.wait()
     for c in ups:
         c.wait_recv()
     join(1)
@@ -335,12 +382,12 @@
     for g in range(3):
         if g < 2:
             join(g + 2)
-        third(g + 1, 1 - ic).wait_recv()
+        arrived(g + 1)
 
         @pl.when(owner)
         def _():
             project_group(g + 1)
-            attend_some([(g, j, 1) for j in range(3)])
+            attend_some([(g, j, half) for half in (1, 0) for j in range(3)])
 
     for c in late:
         c.wait()
@@ -367,7 +414,7 @@
 
     @pl.when(owner)
     def _():
-        attend_some([(3, j, 1) for j in range(3)] + [(g, j, 0) for g in range(G) for j in range(3)])
+        attend_some([(3, j, half) for half in (1, 0) for j in range(3)])
         ctx = jnp.concatenate([ctxt[g].T for g in range(G)], axis=1)
         xh, r = norm(x[...].astype(F32) + nn(ctx, wo[...]))
         xhat1[...] = xh
@@ -419,8 +466,10 @@
                 [gmb if k == 0 else jnp.zeros((16, S), BF), jnp.zeros((48, S), BF)], axis=0
             )
 
-    zsum = [remote(msg.at[i], redz.at[4 - i], gz.at[0, i], gz.at[1, 4 - i], heads=turn(iz, i)) for i in (1, 2, 3)]
-    core_sum = remote(redz.at[0], redc, gc.at[0], gc.at[1], dp_2=1 - ic)
+    zsum = [
+        remote(msg.at[i], redz.at[ic, iz], gz.at[0, o, i], gz.at[1, ic, iz], heads=turn(iz, i), dp_2=turn2(ic, o))
+        for o in (0, 1) for i in range(4) if o + i > 0
+    ]
 
     def line(buf, sem, axis, me):
         return [remote(buf.at[me], buf.at[me], sem.at[0, i], sem.at[1, i], **{axis: turn(me, i)}) for i in (1, 2, 3)]
@@ -436,31 +485,34 @@
         for c in copies:
             c.wait()
 
+    def last_product(half):
+        rows = half_cols(half)
+        igb[rows, :] = (acc[rows, :] + nn(a[rows, 0 : G * GW], wg[...])).astype(BF)
+
     @pl.when(owner)
     def _():
         start(zsum)
-        redz[0] = msg[0]
+        redz[ic, iz] = msg[0]
         for g in range(G):
             a[:, GW * g : GW * g + GW] = dyt[GW * g : GW * g + GW, :].T
-        for half in (1, 0):
-            rows = half_cols(half)
-            igb[rows, :] = (acc[rows, :] + nn(a[rows, 0 : G * GW], wg[...])).astype(BF)
+        last_product(1)
+
+    total = jnp.zeros((32, 256), F32)
+    for c in range(2):
+        for z in range(4):
+            if (z + 2 * c) % 4 != 3:
+                @pl.when(jnp.logical_or(ic != c, iz != z))
+                def _():
+                    pltpu.make_async_copy(msg.at[0], redz.at[c, z], gz.at[1, c, z]).wait()
+                total = total + redz[c, z]
+    redx[ix] = total
+    start(over_x)
+
+    @pl.when(owner)
+    def _():
+        last_product(0)
         back(igb, ig_out, isem)
 
-    @pl.when(rank == 3)
-    def _():
-        redz[0] = jnp.zeros((32, 256), F32)
-
-    for i in (1, 2, 3):
-        @pl.when(turn(rank, i) != 3)
-        def _():
-            pltpu.make_async_copy(msg.at[i], redz.at[i], gz.at[1, i]).wait()
-            redz[0] += redz[i]
-
-    core_sum.start()
-    core_sum.wait()
-    redx[ix] = redz[0] + redc[...]
-    start(over_x)
     finish_copies(over_x)
     redy[iy] = redx[0] + redx[1] + redx[2] + redx[3]
     start(over_y)
@@ -478,17 +530,7 @@
     for c in ups:
         c.wait_send()
 
-    @when_holds
-    def _():
-        for i in (1, 2, 3):
-            over_z(i).wait_send()
-            for k in (1, 2, 3):
-                first(k, i).wait_send()
-
-    for k in (1, 2, 3):
-        for i in (1, 2, 3):
-            second(k, i).wait_send()
-        third(k).wait_send()
+    weights_end()
 
     @pl.when(owner)
     def _():
@@ -509,6 +551,8 @@
 def scratch():
     V, dma = pltpu.VMEM, pltpu.SemaphoreType.DMA
     return [
+        V((B, S), jnp.int32), V((D,), F32), V((D,), F32), V((D,), F32), V((D,), F32),
+        V((8, D), BF), V((8, 192), BF), V((8, D), BF), V((8, 192), BF),
         V((S, D), BF), V((S, D), BF), V((D, D), BF), V((D, FF), BF), V((FF, D), BF), V((G * GW, D), BF),
         V((G, 16, 384), BF), V((S, D), BF), V((S, D), BF),
         V((64, S), BF), V((64, S), BF), V((G, S, 256), BF), V((G, S, 256), BF), V((G, GW, S), BF),
@@ -517,10 +561,10 @@
         V((2, S, C), F32), V((S, FF), BF), V((S, FF), F32), V((S, D), F32),
         V((G, 192, S), F32), V((3, 64, 256), BF), V((3, S, 256), BF), V((12, 2, 64, S), F32), V((G * GW, S), BF),
         V((S, D), BF),
-        V((4, 32, 256), F32), V((4, 32, 256), F32), V((32, 256), F32), V((4, 32, 256), F32), V((4, 32, 256), F32),
+        V((4, 32, 256), F32), V((2, 4, 32, 256), F32), V((4, 32, 256), F32), V((4, 32, 256), F32),
         V((4, 16, 256), F32),
-        dma((6,)), dma((2, 4)), dma((2, 4)), dma((2, 4)), dma((2, 4)), dma((2, 4, 4)), dma((2, 4, 4)), dma((2, 4)),
-        dma((2, 4)), dma((2, 4)), dma((2, 4)), dma((2,)), dma((2, 4)), dma((2, 4)), dma((2, 4)),
+        dma((15,)), dma((2, 4)), dma((2, 4)), dma((2,)), dma((2, 4)), dma((2, 4)), dma((2, 4, 4)), dma((2, 4, 4)),
+        dma((2, 4)), dma((2, 4)), dma((2, 2, 4)), dma((2, 4)), dma((2, 4)), dma((2, 4)),
     ]
 
 
@@ -530,7 +574,7 @@
     act, ig, gd, gu = pl.pallas_call(
         layer,
         out_shape=(shape((B, Q, D), BF), shape((B, Q, D), BF), shape((4, 16, 256), F32), shape((16, 256), F32)),
-        in_specs=[hbm, hbm, vm, pl.BlockSpec(memory_space=pltpu.SMEM)] + [hbm] * 6 + [vm] * 8,
+        in_specs=[hbm] * 3 + [pl.BlockSpec(memory_space=pltpu.SMEM)] + [hbm] * 14,
         out_specs=(hbm, hbm, vm, vm),
         scratch_shapes=scratch(),
         compiler_params=pltpu.CompilerParams(

time: 83.3 us -> 98.4 us (1.18)
  Pallas kernels: 82.2 us -> 96.6 us
    pallas_call x1, Pallas kernels: 79.7 us -> 94 us  [per_device(): pl.pallas_call(layer, out_shape=(shape((B, Q, D), BF), shape((B, Q, D), B...]
where the time goes in v4:
time: 98.4 us; the launch traced here: 97.2 us
  Pallas kernels  96.6 us (98%)
    pallas_call x1, Pallas kernels, per_device(): pl.pallas_call(layer, out_shape=(shape((B, Q, D), BF), shape((B, Q, D), B...  94 us
    pallas_call x1, Pallas kernels, per_device(): pl.pallas_call(finish, out_shape=(shape((B, Q, D), BF), shape((B, Q, D),...  2.56 us

profile of v4, /device:TPU:0, one launch (start us, length us, event | category | flops | bytes accessed | tf_op | source)
XLA Modules:
  0.0 97.2 jit_solution(11101295024565613655)
XLA Ops:
  0.6 94.0 %shard_map.217 = (bf16[3,128,768]{2,1,0:T(8,128)(2,1)}, bf16[3,128,768]{2,1,0:T(8,128)(2,1)}, f32[4,16,256]{2,1,0:T(8,128)}, f32[16,256]{1,0:T(8,128)}) custom-call(bf16[3,128,768]{2,1,0:T(8,128)(2,1)} %inputs.1, bf16[3,128,768]{2,1,0:T(8,128)(2,1)} %cot.1, s32[3,512]{1,0:T(4,128)} %kmask_in.1, s32[3]{0:T(128)} %lengths.1, bf16[192,768]{1,0:T(8,128)(2,1)} %bitcast.7, ...), custom_call_target="tpu_custom_call" | custom-call | tf_op jit(solution)/shard_map/pallas_call | solution.py:574
  94.7 2.6 %shard_map.218 = (bf16[3,128,768]{2,1,0:T(8,128)(2,1)}, f32[3,128,768]{2,1,0:T(8,128)}, f32[8,768]{1,0:T(8,128)}, f32[8,192]{1,0:T(8,128)}, f32[8,768]{1,0:T(8,128)}, /*index=5*/f32[8,192]{1,0:T(8,128)}) custom-call(bf16[3,128,768]{2,1,0:T(8,128)(2,1)} %get-tuple-element.16.act_in, bf16[3,128,768]{2,1,0:T(8,128)(2,1)} %get-tuple-element.17.ig_in, ...), custom_call_target="tpu_custom_call" | custom-call | tf_op jit(solution)/shard_map/pallas_call | solution.py:587

commit v5 on v4

--- a/solution.py
+++ b/solution.py
@@ -91,28 +91,29 @@
     staged(units, scores, weights, mix)
 
 
-def attend_back(units, place, vnat, yt, p, rl, ctxt, dot_ref, dosc, dsscr, dkv, dyt):
-    def grads(u, g, j, half):
-        rows, cols = slice(64 * j, 64 * j + 64), half_cols(half)
-        do = (dot_ref[place(g), rows, cols].astype(F32) * rl[g * 3 + j, :, cols]).astype(BF)
+def attend_back(units, place, vnat, yt, p, rl, ctxt, dot_ref, dosc, dyt, group_done):
+    def values(u, g, j):
+        rows, h = slice(64 * j, 64 * j + 64), g * 3 + j
+        do = (dot_ref[place(g), rows, :] * rl[h]).astype(BF)
         dosc[u % 3] = do
-        dsum = jnp.sum(do.astype(F32) * ctxt[place(g), rows, cols].astype(F32), axis=0, keepdims=True)
-        dp = nn(vnat[g], pad_rows(do, 64 + 64 * j, 256))
-        dsscr[u % 3] = (p[g * 3 + j, :, cols].astype(F32) * (dp - dsum)).astype(BF)
-
-    def products(u, g, j, half):
-        h, cols, at = g * 3 + j, half_cols(half), GW * g + 64 * j
-        ds = dsscr[u % 3]
-        dv = nt(dosc[u % 3], p[h, :, cols])
-        dk = nt(yt[g, 64 * j : 64 * j + 64, cols], ds)
-        dyt[at : at + 64, cols] = (nn(yt[g, 384 + 64 * j : 448 + 64 * j, :], ds) * 0.125).astype(BF)
-        if half == 0:
-            dkv[h, 0], dkv[h, 1] = dv, dk
-        else:
-            dyt[at + 192 : at + 256, :] = (dkv[h, 0] + dv).astype(BF)
-            dyt[at + 384 : at + 448, :] = (dkv[h, 1] + dk).astype(BF)
-
-    staged(units, grads, products)
+        dyt[g, 192 + 64 * j : 256 + 64 * j, :] = nt(do, p[h]).astype(BF)
+
+    def scores(u, g, j):
+        rows, h = slice(64 * j, 64 * j + 64), g * 3 + j
+        for half in range(2):
+            cols = half_cols(half)
+            do = dosc[u % 3, :, cols]
+            dsum = jnp.sum(do.astype(F32) * ctxt[place(g), rows, cols].astype(F32), axis=0, keepdims=True)
+            dp = nn(vnat[g], pad_rows(do, 64 + 64 * j, 256))
+            p[h, :, cols] = (p[h, :, cols].astype(F32) * (dp - dsum)).astype(BF)
+
+    def queries(u, g, j):
+        ds = p[g * 3 + j]
+        dyt[g, 64 * j : 64 * j + 64, :] = (nn(yt[g, 384 + 64 * j : 448 + 64 * j, :], ds) * 0.125).astype(BF)
+        if j == 2:
+            group_done(g)
+
+    staged(units, values, scores, queries)
 
 
 def gelu_pair(v):
@@ -140,14 +141,16 @@
 
 def feed_forward(n1b, wi, wt, hs, a, dact, acc):
     n = FF // C
-    for c in range(n + 1):
+    for c in range(n + 2):
         if c < n:
             hs[c % 2] = nn(n1b[...], wi[:, C * c : C * c + C])
-        if c > 0:
+        if 0 < c <= n:
             cols = slice(C * (c - 1), C * c)
             v, d = gelu_pair(hs[(c - 1) % 2])
             a[:, cols] = v.astype(BF)
             dact[:, cols] = d
+        if c > 1:
+            cols = slice(C * (c - 2), C * (c - 1))
             acc[...] += nn(a[:, cols], wt[cols, :])
 
 
@@ -167,9 +170,9 @@
     act_out, ig_out, gd_out, gu_out,
     kmask, g1, b1, g2, b2, dq, uq, dv, uv, x, ct, wo, wi, wt, wg, up, act, igb,
     bias, mid, knat, vnat, yt, sscr, p, rl, ctxt, xhat1, xhat2, r1s, n1b, hs, a, dact, acc,
-    dot_ref, dosc, dsscr, dkv, dyt, gnb,
-    msg, redz, redx, redy, gdp,
-    lsem, xsem, csem, wsem, usem, w1, w2, w3, asem, isem, gz, gx, gy, gf,
+    dot_ref, dosc, dyt, gnb,
+    msg, redz, redx, redy, gmid,
+    lsem, xsem, csem, wsem, usem, w1, w2, w3, asem, isem, gz, gx, gy,
 ):
     ix, iy, ic, iz = (lax.axis_index(n) for n in ("dp_0", "dp_1", "dp_2", "heads"))
     rank = lax.rem(iz + 2 * ic, 4)
@@ -192,7 +195,8 @@
     peers = [{"dp_2": 1 - ic}]
     for i in (1, 2, 3):
         peers += [{"heads": turn(iz, i)}, {"dp_0": turn(ix, i)}, {"dp_1": turn(iy, i)}]
-    peers += [{"heads": turn(iz, i), "dp_2": 1 - ic} for i in (1, 2, 3)]
+    for i in (1, 2, 3):
+        peers += [{"heads": turn(iz, i), "dp_2": 1 - ic}, {"dp_1": turn(iy, i), "dp_2": 1 - ic}]
     for where in peers:
         pl.semaphore_signal(barrier, inc=1, device_id=where, device_id_type=MESH)
     weights = (wq, wv, wk)
@@ -209,19 +213,19 @@
     ]
     for c in loads + small:
         c.start()
-    pl.semaphore_wait(barrier, 13)
-    for c in loads + small:
+    pl.semaphore_wait(barrier, 16)
+    for c in loads:
         c.wait()
 
     la, lb = ix * (1 - ic) + iy * ic, iy * (1 - ic) + ix * ic
+    holds = la < 3
 
     def part(k, at, count, core=ic):
         rows = pl.ds(pl.multiple_of(GW * k + at, 16), count)
         return wg.at[rows, pl.ds(pl.multiple_of(384 * core, 128), 384)]
 
-    def block(k, b, half=None, core=ic):
-        at, count = ((0, 144), (0, 80), (80, 64))[0 if half is None else half + 1]
-        return part(k, 144 * b + at, count, core)
+    def piece(k, a):
+        return part(k, 48 * (3 * lb + a), 48)
 
     def along_a(i):
         return {"dp_0": turn(ix, i * (1 - ic)), "dp_1": turn(iy, i * ic)}
@@ -229,96 +233,80 @@
     def along_b(i):
         return {"dp_0": turn(ix, i * ic), "dp_1": turn(iy, i * (1 - ic))}
 
-    over_z = remote(block(0, lb), block(la, lb), wsem.at[0], wsem.at[1], heads=turn(iz, 4 - la))
-
-    def ring_a(n, k):
-        what = block(k, lb, n - 2 if n > 1 else None)
-        return remote(what, what, w1.at[0, n], w1.at[1, n], **along_a(3 if n % 2 else 1))
-
-    def ring_b(n, k, b):
-        what = block(k, b, n - 2 if n > 1 else None)
-        return remote(what, what, w2.at[0, n, k], w2.at[1, n, k], **along_b(3 if n % 2 else 1))
-
-    def to_core(k, b, core=ic):
-        what = block(k, b, None, core)
-        return remote(what, what, w3.at[0, k, b], w3.at[1, k, b], dp_2=1 - ic)
-
-    def got_line(k):
-        ring_b(0, k, lb).start()
-        ring_b(1, k, lb).start()
-        to_core(k, lb).start()
+    def over_z(i):
+        return remote(piece(0, la), piece(4 - i, la), wsem.at[0, i], wsem.at[1, 4 - i], heads=turn(iz, i))
+
+    def first(k, i):
+        return remote(piece(k, la), piece(k, la), w1.at[0, k, i], w1.at[1, k, i], **along_a(i))
+
+    def second(k, a, i):
+        return remote(piece(k, a), piece(k, a), w2.at[0, k, a, i], w2.at[1, k, a, i], **along_b(i))
+
+    def third(k, core=ic):
+        what = part(k, 0, 576, core)
+        return remote(what, what, w3.at[0, k], w3.at[1, k], dp_2=1 - ic)
 
     def join_line():
-        @pl.when(la > 0)
+        @pl.when(holds)
         def _():
-            over_z.wait_recv()
-            ring_a(0, la).start()
-            ring_a(1, la).start()
-            got_line(la)
-
-        for n, k in ((0, turn(la, 3)), (1, turn(la, 1))):
-            @pl.when(k > 0)
-            def _():
-                ring_a(n, k).wait_recv()
-                ring_a(n + 2, k).start()
-                got_line(k)
-
-        far = turn(la, 2)
-
-        @pl.when(far > 0)
+            for k in (1, 2, 3):
+                over_z(4 - k).wait_recv()
+                for i in (1, 2, 3):
+                    first(k, i).start()
+                    second(k, la, i).start()
+
+        for k in (1, 2, 3):
+            for i in (1, 2, 3):
+                source = turn(la, 4 - i)
+
+                @pl.when(source < 3)
+                def _():
+                    first(k, i).wait_recv()
+                    for n in (1, 2, 3):
+                        second(k, source, n).start()
+
+    def join(k):
+        for a in range(3):
+            for i in (1, 2, 3):
+                second(k, a, i).wait_recv()
+        third(k).start()
+
+    def arrived(k):
+        third(k, 1 - ic).wait_recv()
+
+    def weights_end():
+        @pl.when(holds)
         def _():
-            ring_a(2, far).wait_recv()
-            ring_a(3, far).wait_recv()
-            got_line(far)
-
-    def join(k):
-        for n, b in ((0, turn(lb, 3)), (1, turn(lb, 1))):
-            ring_b(n, k, b).wait_recv()
-            ring_b(n + 2, k, b).start()
-            to_core(k, b).start()
-        far = turn(lb, 2)
-        ring_b(2, k, far).wait_recv()
-        ring_b(3, k, far).wait_recv()
-        to_core(k, far).start()
-
-    def arrived(k):
-        for b in range(4):
-            to_core(k, b, 1 - ic).wait_recv()
-
-    def weights_end():
-        @pl.when(la > 0)
-        def _():
-            over_z.wait_send()
-            ring_a(0, la).wait_send()
-            ring_a(1, la).wait_send()
-
-        for n, k in ((0, turn(la, 3)), (1, turn(la, 1))):
-            @pl.when(k > 0)
-            def _():
-                ring_a(n + 2, k).wait_send()
+            for i in (1, 2, 3):
+                over_z(i).wait_send()
+                for k in (1, 2, 3):
+                    first(k, i).wait_send()
 
         for k in (1, 2, 3):
-            for n in range(4):
-                ring_b(n, k, lb).wait_send()
-            for b in range(4):
-                to_core(k, b).wait_send()
-
-    @pl.when(la > 0)
-    def _():
-        over_z.start()
+            for a in range(3):
+                for i in (1, 2, 3):
+                    second(k, a, i).wait_send()
+            third(k).wait_send()
+
+    @pl.when(holds)
+    def _():
+        for i in (1, 3, 2):
+            over_z(i).start()
 
     def slot(ref, r):
         return ref.at[pl.ds(pl.multiple_of(r * Q, Q), Q)]
 
+    def spread_to(src, dst, sem, i):
+        j = jnp.minimum(turn(rank, i), 2)
+        return remote(src.at[j], slot(dst, rank), sem.at[0, i], sem.at[1, rank], heads=turn(iz, i))
+
     def spread(src, dst, sem):
-        for j in range(B):
-            @pl.when(rank != j)
-            def _():
-                remote(src.at[j], slot(dst, rank), sem.at[0, j], sem.at[1, rank], heads=z_of(j)).start()
-
-            @pl.when(rank == j)
-            def _():
-                pltpu.make_async_copy(src.at[j], slot(dst, rank), sem.at[1, j]).start()
+        for i in (2, 1, 3):
+            pl.when(turn(rank, i) < 3)(spread_to(src, dst, sem, i).start)
+
+        @pl.when(owner)
+        def _():
+            pltpu.make_async_copy(src.at[mine], slot(dst, mine), sem.at[1, mine]).start()
 
     def spread_wait(src, dst, sem):
         @pl.when(owner)
@@ -327,13 +315,13 @@
                 pltpu.make_async_copy(src.at[0], dst.at[pl.ds(r * Q, Q)], sem.at[1, r]).wait()
 
     def spread_end(src, dst, sem):
-        for j in range(B):
-            @pl.when(rank != j)
-            def _():
-                remote(src.at[j], slot(dst, rank), sem.at[0, j], sem.at[1, rank], heads=z_of(j)).wait_send()
+        for i in (1, 2, 3):
+            pl.when(turn(rank, i) < 3)(spread_to(src, dst, sem, i).wait_send)
 
     spread(inputs, x, xsem)
 
+    for c in small:
+        c.wait()
     zero8 = jnp.zeros((8, 192), F32)
     both = jnp.concatenate(
         [
@@ -398,10 +386,13 @@
     def sent_back(src, dst, sem, i):
         return remote(rows_of(src, turn(rank, i)), dst.at[mine], sem.at[0, i], sem.at[1, mine], heads=turn(iz, i))
 
+    def own_back(src, dst, sem):
+        return pltpu.make_async_copy(rows_of(src, mine), dst.at[mine], sem.at[1, mine])
+
     def back(src, dst, sem):
         for i in (1, 2, 3):
             sent_back(src, dst, sem, i).start()
-        pltpu.make_async_copy(rows_of(src, mine), dst.at[mine], sem.at[1, mine]).start()
+        own_back(src, dst, sem).start()
 
     def back_end(src, dst, sem):
         for j in range(B):
@@ -446,36 +437,37 @@
         gfb = gf1.astype(BF)
         for g in range(G):
             dot_ref[g] = nt(wo[192 * g : 192 * g + 192, :], gfb)
-        for half in range(2):
-            attend_back([(g, j, half) for g in range(G) for j in range(3)], place, vnat, yt, p, rl, ctxt, dot_ref, dosc,
-                        dsscr, dkv, dyt)
-        gm = jnp.zeros((16, S), F32)
+        middle_sum = [jnp.zeros((16, S), F32)]
         first_rows = lax.broadcasted_iota(jnp.int32, (16, 192), 0) < 8
+
+        def group_done(g):
+            dqv = dyt[g]
+            a[:, GW * g : GW * g + 384] = dqv.T
+            gu = nt(mid[0:16, :], dqv)
+            gu = jnp.where(first_rows, gu[:, 0:192], gu[:, 192:384]) * 2.0
+            msg[g, 1, :, 256:512] = jnp.concatenate([gu, jnp.zeros((16, 64), F32)], axis=1).astype(BF)
+            middle_sum[0] = middle_sum[0] + nn(up[g], dqv)
+
+        attend_back([(g, j) for g in range(G) for j in range(3)], place, vnat, yt, p, rl, ctxt, dot_ref, dosc, dyt, group_done)
+        gmb = middle_sum[0].astype(BF)
+        gmid[0:16, :] = gmb
+        gmid[16:64, :] = jnp.zeros((48, S), BF)
+        gd = nn(gmb, x[...]).astype(BF)
         for g in range(G):
-            dqv = dyt[GW * g : GW * g + 384, :]
-            gu = nt(mid[0:16, :], dqv)
-            msg[g, 0:16, 0:192] = jnp.where(first_rows, gu[:, 0:192], gu[:, 192:384]) * 2.0
-            gm = gm + nn(up[g], dqv)
-        gmb = gm.astype(BF)
-        gd = nn(gmb, x[...])
-        for q in range(4):
-            gdp[q, :, 0:192] = gd[:, 192 * q : 192 * q + 192]
-        for k in range(G):
-            msg[k, 16:32, 0:192] = gdp[place(k), :, 0:192]
-            dyt[GW * k + 576 : GW * k + GW, :] = jnp.concatenate(
-                [gmb if k == 0 else jnp.zeros((16, S), BF), jnp.zeros((48, S), BF)], axis=0
-            )
+            msg[g, 0] = gd[:, 0:512]
+            msg[g, 1, :, 0:256] = gd[:, 512:768]
 
     zsum = [
-        remote(msg.at[i], redz.at[ic, iz], gz.at[0, o, i], gz.at[1, ic, iz], heads=turn(iz, i), dp_2=turn2(ic, o))
+        remote(msg.at[i, turn2(ic, o)], redz.at[ic, iz], gz.at[0, o, i], gz.at[1, ic, iz], heads=turn(iz, i), dp_2=turn2(ic, o))
         for o in (0, 1) for i in range(4) if o + i > 0
     ]
-
-    def line(buf, sem, axis, me):
-        return [remote(buf.at[me], buf.at[me], sem.at[0, i], sem.at[1, i], **{axis: turn(me, i)}) for i in (1, 2, 3)]
-
-    over_x, over_y = line(redx, gx, "dp_0", ix), line(redy, gy, "dp_1", iy)
-    over_q = [remote(gd_out.at[iz], gd_out.at[iz], gf.at[0, i], gf.at[1, i], heads=turn(iz, i)) for i in (1, 2, 3)]
+    over_x = [
+        remote(redx.at[ix], redx.at[ix], gx.at[0, i], gx.at[1, i], dp_0=turn(ix, i)) for i in (1, 2, 3)
+    ]
+    over_y = [
+        remote(redy.at[ic, iy], redy.at[ic, iy], gy.at[0, o, i], gy.at[1, ic, iy], dp_1=turn(iy, i), dp_2=turn2(ic, o))
+        for o in (0, 1) for i in range(4) if o + i > 0
+    ]
 
     def start(copies):
         for c in copies:
@@ -485,43 +477,58 @@
         for c in copies:
             c.wait()
 
-    def last_product(half):
-        rows = half_cols(half)
+    def last_product(i):
+        rows = pl.ds(pl.multiple_of(turn(rank, i) * Q, Q), Q)
+        for g in range(G):
+            dk = [nt(yt[g, 64 * j : 64 * j + 64, :], p[3 * g + j, rows, :]).astype(BF) for j in range(3)]
+            tail = gmid[:, rows] if g == 0 else jnp.zeros((64, Q), BF)
+            a[rows, GW * g + 384 : GW * g + GW] = jnp.concatenate(dk + [tail], axis=0).T
         igb[rows, :] = (acc[rows, :] + nn(a[rows, 0 : G * GW], wg[...])).astype(BF)
+        if i:
+            sent_back(igb, ig_out, isem, i).start()
 
     @pl.when(owner)
     def _():
         start(zsum)
-        redz[ic, iz] = msg[0]
-        for g in range(G):
-            a[:, GW * g : GW * g + GW] = dyt[GW * g : GW * g + GW, :].T
-        last_product(1)
-
-    total = jnp.zeros((32, 256), F32)
+        redz[ic, iz] = msg[0, ic]
+        last_product(2)
+
+    def from_others(buf, sem, c, n, me):
+        @pl.when(jnp.logical_or(ic != c, me != n))
+        def _():
+            pltpu.make_async_copy(redx.at[0], buf.at[c, n], sem.at[1, c, n]).wait()
+
+    total = jnp.zeros((16, 512), F32)
     for c in range(2):
         for z in range(4):
             if (z + 2 * c) % 4 != 3:
-                @pl.when(jnp.logical_or(ic != c, iz != z))
-                def _():
-                    pltpu.make_async_copy(msg.at[0], redz.at[c, z], gz.at[1, c, z]).wait()
-                total = total + redz[c, z]
-    redx[ix] = total
+                from_others(redz, gz, c, z, iz)
+                total = total + redz[c, z].astype(F32)
+    redx[ix] = total.astype(BF)
     start(over_x)
 
     @pl.when(owner)
     def _():
+        last_product(1)
+
+    finish_copies(over_x)
+    redy[ic, iy] = sum(redx[n].astype(F32) for n in range(4)).astype(BF)
+    start(over_y)
+
+    @pl.when(owner)
+    def _():
+        last_product(3)
         last_product(0)
-        back(igb, ig_out, isem)
-
-    finish_copies(over_x)
-    redy[iy] = redx[0] + redx[1] + redx[2] + redx[3]
-    start(over_y)
-    finish_copies(over_y)
-    total = redy[0] + redy[1] + redy[2] + redy[3]
-    gu_out[...] = total[0:16]
-    gd_out[iz] = total[16:32]
-    start(over_q)
-    finish_copies(over_q)
+        own_back(igb, ig_out, isem).start()
+
+    halves = []
+    for c in range(2):
+        for n in range(4):
+            from_others(redy, gy, c, n, iy)
+        halves.append(sum(redy[c, n].astype(F32) for n in range(4)))
+    gd_out[:, 0:512] = halves[0]
+    gd_out[:, 512:768] = halves[1][:, 0:256]
+    gu_out[...] = halves[1][:, 256:448]
 
     back_end(act, act_out, asem)
     back_end(igb, ig_out, isem)
@@ -532,6 +539,9 @@
 
     weights_end()
 
+    for c in over_y:
+        c.wait_send()
+
     @pl.when(owner)
     def _():
         for c in zsum:
@@ -541,11 +551,10 @@
 def finish(act_in, ig_in, gd, gu, act, ig, gdq, guq, gdv, guv):
     act[...] = act_in[...]
     ig[...] = ig_in[...].astype(F32)
-    down = jnp.concatenate([gd[q, :, 0:192] for q in range(4)], axis=1)
-    gdq[...] = down[0:8]
-    gdv[...] = down[8:16]
-    guq[...] = gu[0:8, 0:192]
-    guv[...] = gu[8:16, 0:192]
+    gdq[...] = gd[0:8, :]
+    gdv[...] = gd[8:16, :]
+    guq[...] = gu[0:8, :]
+    guv[...] = gu[8:16, :]
 
 
 def scratch():
@@ -559,12 +568,12 @@
         V((3, S, 256), F32), V((12, S, S), BF), V((12, 1, S), F32), V((G, 192, S), BF),
         V((S, D), F32), V((S, D), F32), V((S, 1), F32), V((S, D), BF),
         V((2, S, C), F32), V((S, FF), BF), V((S, FF), F32), V((S, D), F32),
-        V((G, 192, S), F32), V((3, 64, 256), BF), V((3, S, 256), BF), V((12, 2, 64, S), F32), V((G * GW, S), BF),
+        V((G, 192, S), F32), V((3, 64, S), BF), V((G, 384, S), BF),
         V((S, D), BF),
-        V((4, 32, 256), F32), V((2, 4, 32, 256), F32), V((4, 32, 256), F32), V((4, 32, 256), F32),
-        V((4, 16, 256), F32),
-        dma((15,)), dma((2, 4)), dma((2, 4)), dma((2,)), dma((2, 4)), dma((2, 4)), dma((2, 4, 4)), dma((2, 4, 4)),
-        dma((2, 4)), dma((2, 4)), dma((2, 2, 4)), dma((2, 4)), dma((2, 4)), dma((2, 4)),
+        V((4, 2, 16, 512), BF), V((2, 4, 16, 512), BF), V((4, 16, 512), BF), V((2, 4, 16, 512), BF),
+        V((64, S), BF),
+        dma((15,)), dma((2, 4)), dma((2, 4)), dma((2, 4)), dma((2, 4)), dma((2, 4, 4)), dma((2, 4, 3, 4)), dma((2, 4)),
+        dma((2, 4)), dma((2, 4)), dma((2, 2, 4)), dma((2, 4)), dma((2, 2, 4)),
     ]
 
 
@@ -573,7 +582,7 @@
     shape = jax.ShapeDtypeStruct
     act, ig, gd, gu = pl.pallas_call(
         layer,
-        out_shape=(shape((B, Q, D), BF), shape((B, Q, D), BF), shape((4, 16, 256), F32), shape((16, 256), F32)),
+        out_shape=(shape((B, Q, D), BF), shape((B, Q, D), BF), shape((16, D), F32), shape((16, 192), F32)),
         in_specs=[hbm] * 3 + [pl.BlockSpec(memory_space=pltpu.SMEM)] + [hbm] * 14,
         out_specs=(hbm, hbm, vm, vm),
         scratch_shapes=scratch(),

time: 98.4 us -> 79.2 us (0.80); the launches traced: 97.2 us -> 79.1 us
  Pallas kernels: 96.6 us -> 78.4 us
    pallas_call x1, Pallas kernels: 94 us -> 75.8 us  [per_device(): pl.pallas_call(layer, out_shape=(shape((B, Q, D), BF), shape((B, Q, D), B...]
where the time goes in v5:
time: 79.2 us; the launch traced here: 79.1 us
  Pallas kernels  78.4 us (99%)
    pallas_call x1, Pallas kernels, per_device(): pl.pallas_call(layer, out_shape=(shape((B, Q, D), BF), shape((B, Q, D), B...  75.8 us
    pallas_call x1, Pallas kernels, per_device(): pl.pallas_call(finish, out_shape=(shape((B, Q, D), BF), shape((B, Q, D),...  2.56 us

profile of v5, /device:TPU:0, one launch (start us, length us, event | category | flops | bytes accessed | tf_op | source)
XLA Modules:
  0.0 79.1 jit_solution(3928993970486864131)
XLA Ops:
  0.6 75.8 %shard_map.217 = (bf16[3,128,768]{2,1,0:T(8,128)(2,1)}, bf16[3,128,768]{2,1,0:T(8,128)(2,1)}, f32[16,768]{1,0:T(8,128)}, f32[16,192]{1,0:T(8,128)}) custom-call(bf16[3,128,768]{2,1,0:T(8,128)(2,1)} %inputs.1, bf16[3,128,768]{2,1,0:T(8,128)(2,1)} %cot.1, s32[3,512]{1,0:T(4,128)} %kmask_in.1, s32[3]{0:T(128)} %lengths.1, bf16[192,768]{1,0:T(8,128)(2,1)} %bitcast.7, ...), custom_call_target="tpu_custom_call" | custom-call | tf_op jit(solution)/shard_map/pallas_call | solution.py:583
  76.5 2.6 %shard_map.218 = (bf16[3,128,768]{2,1,0:T(8,128)(2,1)}, f32[3,128,768]{2,1,0:T(8,128)}, f32[8,768]{1,0:T(8,128)}, f32[8,192]{1,0:T(8,128)}, f32[8,768]{1,0:T(8,128)}, /*index=5*/f32[8,192]{1,0:T(8,128)}) custom-call(bf16[3,128,768]{2,1,0:T(8,128)(2,1)} %get-tuple-element.16.act_in, bf16[3,128,768]{2,1,0:T(8,128)(2,1)} %get-tuple-element.17.ig_in, ...), custom_call_target="tpu_custom_call" | custom-call | tf_op jit(solution)/shard_map/pallas_call | solution.py:596

commit v6 on v5

--- a/solution.py
+++ b/solution.py
@@ -159,6 +159,9 @@
         cols = slice(C * c, C * c + C)
         a[:, cols] = (nt(gnb[...], wt[cols, :]) * dact[:, cols]).astype(BF)
     acc[...] += nt(a[...], wi[...])
+NEAR = (1, 3, 2)
+
+
 def remote(src, dst, send, recv, **where):
     return pltpu.make_async_remote_copy(
         src_ref=src, dst_ref=dst, send_sem=send, recv_sem=recv, device_id=where, device_id_type=MESH
@@ -249,20 +252,21 @@
     def join_line():
         @pl.when(holds)
         def _():
-            for k in (1, 2, 3):
+            for k in NEAR:
                 over_z(4 - k).wait_recv()
-                for i in (1, 2, 3):
+                for i in NEAR:
                     first(k, i).start()
+                for i in NEAR:
                     second(k, la, i).start()
 
-        for k in (1, 2, 3):
-            for i in (1, 2, 3):
+        for k in NEAR:
+            for i in NEAR:
                 source = turn(la, 4 - i)
 
                 @pl.when(source < 3)
                 def _():
                     first(k, i).wait_recv()
-                    for n in (1, 2, 3):
+                    for n in NEAR:
                         second(k, source, n).start()
 
     def join(k):
@@ -343,7 +347,6 @@
         )
 
     join_line()
-    spread(cot, ct, csem)
     for c in late:
         c.start()
 
@@ -353,8 +356,9 @@
     bias[...] = jnp.where(lax.broadcasted_iota(jnp.int32, (64, S), 0) == 63, row, 0.0).astype(BF)
     for c in ups:
         c.wait_recv()
-    join(1)
     spread_wait(inputs, x, xsem)
+    spread_end(inputs, x, xsem)
+    spread(cot, ct, csem)
 
     def project_group(g):
         project(g, x, wg, up, mid, bias, knat, vnat, yt)
@@ -362,20 +366,31 @@
     def attend_some(units):
         attend(units, place, knat, yt, sscr, p, rl, ctxt)
 
+    def all_of(g):
+        return [(g, j, half) for half in (1, 0) for j in range(3)]
+
+    order = (0,) + NEAR
+
     @pl.when(owner)
     def _():
         middle(x, wg, mid)
         project_group(0)
 
-    for g in range(3):
-        if g < 2:
-            join(g + 2)
-        arrived(g + 1)
+    join(order[1])
+
+    @pl.when(owner)
+    def _():
+        attend_some(all_of(0))
+
+    for n in range(3):
+        if n < 2:
+            join(order[n + 2])
+        arrived(order[n + 1])
 
         @pl.when(owner)
         def _():
-            project_group(g + 1)
-            attend_some([(g, j, half) for half in (1, 0) for j in range(3)])
+            project_group(order[n + 1])
+            attend_some(all_of(order[n + 1]))
 
     for c in late:
         c.wait()
@@ -405,7 +420,6 @@
 
     @pl.when(owner)
     def _():
-        attend_some([(3, j, half) for half in (1, 0) for j in range(3)])
         ctx = jnp.concatenate([ctxt[g].T for g in range(G)], axis=1)
         xh, r = norm(x[...].astype(F32) + nn(ctx, wo[...]))
         xhat1[...] = xh
@@ -492,6 +506,7 @@
         start(zsum)
         redz[ic, iz] = msg[0, ic]
         last_product(2)
+        last_product(1)
 
     def from_others(buf, sem, c, n, me):
         @pl.when(jnp.logical_or(ic != c, me != n))
@@ -509,7 +524,7 @@
 
     @pl.when(owner)
     def _():
-        last_product(1)
+        last_product(3)
 
     finish_copies(over_x)
     redy[ic, iy] = sum(redx[n].astype(F32) for n in range(4)).astype(BF)
@@ -517,7 +532,6 @@
 
     @pl.when(owner)
     def _():
-        last_product(3)
         last_product(0)
         own_back(igb, ig_out, isem).start()
 
@@ -532,7 +546,6 @@
 
     back_end(act, act_out, asem)
     back_end(igb, ig_out, isem)
-    spread_end(inputs, x, xsem)
     spread_end(cot, ct, csem)
     for c in ups:
         c.wait_send()

time: 79.2 us -> 74.2 us (0.937); the launches traced: 79.1 us -> 73 us
  Pallas kernels: 78.4 us -> 72.3 us
    pallas_call x1, Pallas kernels: 75.8 us -> 69.8 us  [per_device(): pl.pallas_call(layer, out_shape=(shape((B, Q, D), BF), shape((B, Q, D), B...]
where the time goes in v6:
time: 74.2 us; the launch traced here: 73 us
  Pallas kernels  72.3 us (97%)
    pallas_call x1, Pallas kernels, per_device(): pl.pallas_call(layer, out_shape=(shape((B, Q, D), BF), shape((B, Q, D), B...  69.8 us
    pallas_call x1, Pallas kernels, per_device(): pl.pallas_call(finish, out_shape=(shape((B, Q, D), BF), shape((B, Q, D),...  2.56 us

profile of v6, /device:TPU:0, one launch (start us, length us, event | category | flops | bytes accessed | tf_op | source)
XLA Modules:
  0.0 73.0 jit_solution(2297215481653757461)
XLA Ops:
  0.6 69.8 %shard_map.217 = (bf16[3,128,768]{2,1,0:T(8,128)(2,1)}, bf16[3,128,768]{2,1,0:T(8,128)(2,1)}, f32[16,768]{1,0:T(8,128)}, f32[16,192]{1,0:T(8,128)}) custom-call(bf16[3,128,768]{2,1,0:T(8,128)(2,1)} %inputs.1, bf16[3,128,768]{2,1,0:T(8,128)(2,1)} %cot.1, s32[3,512]{1,0:T(4,128)} %kmask_in.1, s32[3]{0:T(128)} %lengths.1, bf16[192,768]{1,0:T(8,128)(2,1)} %bitcast.7, ...), custom_call_target="tpu_custom_call" | custom-call | tf_op jit(solution)/shard_map/pallas_call | solution.py:596
  70.4 2.6 %shard_map.218 = (bf16[3,128,768]{2,1,0:T(8,128)(2,1)}, f32[3,128,768]{2,1,0:T(8,128)}, f32[8,768]{1,0:T(8,128)}, f32[8,192]{1,0:T(8,128)}, f32[8,768]{1,0:T(8,128)}, /*index=5*/f32[8,192]{1,0:T(8,128)}) custom-call(bf16[3,128,768]{2,1,0:T(8,128)(2,1)} %get-tuple-element.16.act_in, bf16[3,128,768]{2,1,0:T(8,128)(2,1)} %get-tuple-element.17.ig_in, ...), custom_call_target="tpu_custom_call" | custom-call | tf_op jit(solution)/shard_map/pallas_call | solution.py:609

commit v7 on v6

--- a/solution.py
+++ b/solution.py
@@ -117,7 +117,7 @@
 
 
 def gelu_pair(v):
-    e = jnp.exp(v * v * -0.5)
+    e = jnp.exp2(v * (v * -0.7213475204444817))
     t = 1.0 / (1.0 + 0.23164189 * jnp.abs(v))
     tail = t * (0.127414796 + t * (-0.142248368 + t * (0.7107068705 + t * (-0.7265760135 + t * 0.5307027145)))) * e
     cdf = jnp.where(v >= 0.0, 1.0 - tail, tail)
@@ -347,8 +347,6 @@
         )
 
     join_line()
-    for c in late:
-        c.start()
 
     row = jnp.where(mine == 0, kmask[0:1], jnp.where(mine == 1, kmask[1:2], kmask[2:3]))
     row = jnp.where(ic == 0, row, jnp.concatenate([row[:, 256:512], row[:, 0:256]], axis=1))
@@ -357,25 +355,27 @@
     for c in ups:
         c.wait_recv()
     spread_wait(inputs, x, xsem)
+
+    def project_group(g):
+        project(g, x, wg, up, mid, bias, knat, vnat, yt)
+
+    def attend_some(units):
+        attend(units, place, knat, yt, sscr, p, rl, ctxt)
+
+    def all_of(g):
+        return [(g, j, half) for half in (1, 0) for j in range(3)]
+
+    order = (0,) + NEAR
+
+    @pl.when(owner)
+    def _():
+        middle(x, wg, mid)
+        project_group(0)
+
     spread_end(inputs, x, xsem)
     spread(cot, ct, csem)
-
-    def project_group(g):
-        project(g, x, wg, up, mid, bias, knat, vnat, yt)
-
-    def attend_some(units):
-        attend(units, place, knat, yt, sscr, p, rl, ctxt)
-
-    def all_of(g):
-        return [(g, j, half) for half in (1, 0) for j in range(3)]
-
-    order = (0,) + NEAR
-
-    @pl.when(owner)
-    def _():
-        middle(x, wg, mid)
-        project_group(0)
-
+    for c in late:
+        c.start()
     join(order[1])
 
     @pl.when(owner)
@@ -449,8 +449,9 @@
         gf1 = norm_back(acc[...] * g1[...][None], xhat1[...], r1s[...])
         acc[...] = gf1
         gfb = gf1.astype(BF)
+        context_grad = nt(wo[...], gfb)
         for g in range(G):
-            dot_ref[g] = nt(wo[192 * g : 192 * g + 192, :], gfb)
+            dot_ref[g] = context_grad[192 * g : 192 * g + 192]
         middle_sum = [jnp.zeros((16, S), F32)]
         first_rows = lax.broadcasted_iota(jnp.int32, (16, 192), 0) < 8
 

time: 74.2 us -> 73.7 us (level)
  no operation moved by 1% of the time
where the time goes in v7:
time: 73.7 us; the launch traced here: 72.4 us
  Pallas kernels  71.8 us (97%)
    pallas_call x1, Pallas kernels, per_device(): pl.pallas_call(layer, out_shape=(shape((B, Q, D), BF), shape((B, Q, D), B...  69.2 us
    pallas_call x1, Pallas kernels, per_device(): pl.pallas_call(finish, out_shape=(shape((B, Q, D), BF), shape((B, Q, D),...  2.56 us

profile of v7, /device:TPU:0, one launch (start us, length us, event | category | flops | bytes accessed | tf_op | source)
XLA Modules:
  0.0 72.4 jit_solution(6716416010896928958)
XLA Ops:
  0.6 69.2 %shard_map.217 = (bf16[3,128,768]{2,1,0:T(8,128)(2,1)}, bf16[3,128,768]{2,1,0:T(8,128)(2,1)}, f32[16,768]{1,0:T(8,128)}, f32[16,192]{1,0:T(8,128)}) custom-call(bf16[3,128,768]{2,1,0:T(8,128)(2,1)} %inputs.1, bf16[3,128,768]{2,1,0:T(8,128)(2,1)} %cot.1, s32[3,512]{1,0:T(4,128)} %kmask_in.1, s32[3]{0:T(128)} %lengths.1, bf16[192,768]{1,0:T(8,128)(2,1)} %bitcast.7, ...), custom_call_target="tpu_custom_call" | custom-call | tf_op jit(solution)/shard_map/pallas_call | solution.py:597
  69.9 2.6 %shard_map.218 = (bf16[3,128,768]{2,1,0:T(8,128)(2,1)}, f32[3,128,768]{2,1,0:T(8,128)}, f32[8,768]{1,0:T(8,128)}, f32[8,192]{1,0:T(8,128)}, f32[8,768]{1,0:T(8,128)}, /*index=5*/f32[8,192]{1,0:T(8,128)}) custom-call(bf16[3,128,768]{2,1,0:T(8,128)(2,1)} %get-tuple-element.16.act_in, bf16[3,128,768]{2,1,0:T(8,128)(2,1)} %get-tuple-element.17.ig_in, ...), custom_call_target="tpu_custom_call" | custom-call | tf_op jit(solution)/shard_map/pallas_call | solution.py:610
